TPU v7x, 128 devices: a whole 4x4x4 slice. The times are simulated.
128 devices in a mesh: section: 2 (over z_hi), ctx: 2 (over z_lo), fsdp: 32 (over y, x, core).
Axes of the slice: x: 4, y: 4, z: 4 (z_hi: 2, z_lo: 2; z = z_hi * 2 + z_lo), core: 2. Of those that a mesh axis runs over, the one named last changes fastest.
Arguments:
- inputs: bfloat16 [2, 32, 256, 1024], P(None, 'fsdp', 'ctx'), may hold values from -6 to 6
- cotangent: bfloat16 [2, 32, 256, 1024], P(None, 'fsdp', 'ctx'), may hold values from -6 to 6
- segments: int32 [2, 32, 256], P(None, 'fsdp'), may hold values from 0 to 3, as said below
- positions: int32 [2, 32, 256], P(None, 'fsdp', 'ctx'), may hold values from 0 to 767, as said below
- attention_gain: bfloat16 [2, 1024], P('section', 'fsdp'), may hold values from 0.5 to 1.5
- attention_bias: bfloat16 [2, 1024], P('section', 'fsdp'), may hold values from -2 to 2
- joint_weight: bfloat16 [2, 1024, 3072], P('section', 'fsdp'), may hold values from -0.1875 to 0.1875
- joint_bias: bfloat16 [2, 3072], P('section', 'fsdp'), may hold values from -2 to 2
- output_weight: bfloat16 [2, 1024, 1024], P('section', 'fsdp'), may hold values from -0.5 to 0.5
- output_bias: bfloat16 [2, 1024], P('section', 'fsdp'), may hold values from -2 to 2
- feed_gain: bfloat16 [2, 1024], P('section', 'fsdp'), may hold values from 0.5 to 1.5
- feed_bias: bfloat16 [2, 1024], P('section', 'fsdp'), may hold values from -2 to 2
- up_weight: bfloat16 [2, 1024, 4096], P('section', 'fsdp'), may hold values from -0.1875 to 0.1875
- up_bias: bfloat16 [2, 4096], P('section', 'fsdp'), may hold values from -2 to 2
- down_weight: bfloat16 [2, 4096, 1024], P('section', 'fsdp'), may hold values from -0.09375 to 0.09375
- down_bias: bfloat16 [2, 1024], P('section', 'fsdp'), may hold values from -2 to 2
Outputs:
- section_out: bfloat16 [2, 2, 32, 256, 1024], P('section', None, 'fsdp', 'ctx')
- input_grad: bfloat16 [2, 2, 32, 256, 1024], P('section', None, 'fsdp', 'ctx')
- attention_gain_grad: float32 [2, 1024], P('section', 'fsdp')
- attention_bias_grad: float32 [2, 1024], P('section', 'fsdp')
- joint_weight_grad: float32 [2, 1024, 3072], P('section', 'fsdp')
- joint_bias_grad: float32 [2, 3072], P('section', 'fsdp')
- output_weight_grad: float32 [2, 1024, 1024], P('section', 'fsdp')
- output_bias_grad: float32 [2, 1024], P('section', 'fsdp')
- feed_gain_grad: float32 [2, 1024], P('section', 'fsdp')
- feed_bias_grad: float32 [2, 1024], P('section', 'fsdp')
- up_weight_grad: float32 [2, 1024, 4096], P('section', 'fsdp')
- up_bias_grad: float32 [2, 4096], P('section', 'fsdp')
- down_weight_grad: float32 [2, 4096, 1024], P('section', 'fsdp')
- down_bias_grad: float32 [2, 1024], P('section', 'fsdp')
Inputs may be any that keep to these rules, and one draw needn't show every extreme that they name: `segments`: document numbers of a sequence start at 0 and rise by one at each new document; every sequence has the same number of documents, and its last one carries the largest number allowed; one document of every sequence holds tokens 256 / 2 - 1 and 128. Within a document positions rise by one from token to token; the last token of every sequence has position 767.
All inputs are finite; a program needn't handle non-finite values.
Results may differ from a plain program's by a relative error of at most 0.024.
Values may be sent and summed in bfloat16 or wider, within the bound.
No kernel may reach another device: no remote copies, remote signals or barrier semaphores. Data moves between devices by JAX's collectives and lax.ppermute only.
A program may use at most 192 MiB of HBM per device.

v0:
```python
import math

import jax
import jax.numpy as jnp
from jax import lax
from jax.sharding import PartitionSpec as P

D = 1024
HEADS = 16
HEAD_DIM = 64
ROT = 16


EPSILON = 1e-05


def from_behind(block, axis, distance):
    devices = range(lax.axis_size(axis))
    route = [(i - distance, i) for i in devices if i - distance in devices]
    return lax.ppermute(block, axis, route)


def norm_parts(resid, gain, bias):
    centred = resid - jnp.mean(resid, -1, keepdims=True)
    scale = lax.rsqrt(jnp.mean(centred * centred, -1, keepdims=True) + EPSILON)
    normed = centred * scale
    return (normed * gain + bias, normed, scale)


def norm_back(incoming, normed, scale, gain):
    inner = incoming * gain.astype(jnp.float32)
    return scale * (
        inner
        - jnp.mean(inner, -1, keepdims=True)
        - normed * jnp.mean(inner * normed, -1, keepdims=True)
    )


def gelu_value(upward):
    return 0.5 * upward * (1.0 + jax.scipy.special.erf(upward * math.sqrt(0.5)))


def gelu_slope(upward):
    return 0.5 * (1.0 + jax.scipy.special.erf(upward * math.sqrt(0.5))) + upward * jnp.exp(
        -0.5 * upward * upward
    ) * math.sqrt(0.5 / math.pi)


def turn_heads(heads, cosine, sine, sign):
    half = cosine.shape[-1]
    first = heads[..., :half]
    second = heads[..., half : 2 * half]
    return jnp.concatenate(
        [
            first * cosine - sign * second * sine,
            second * cosine + sign * first * sine,
            heads[..., 2 * half :],
        ],
        -1,
    )


def contract(left, right):
    return lax.dot_general(
        left, right, (((0,), (0,)), ((), ())), preferred_element_type=jnp.float32
    )


def back_dot(left, weight):
    return lax.dot_general(
        left, weight, (((1,), (1,)), ((), ())), preferred_element_type=jnp.float32
    )


def allowed_mask(seg_whole, place, rows):
    total_len = seg_whole.shape[0]
    seg_query = lax.dynamic_slice_in_dim(seg_whole, place * rows, rows)
    query_index = place * rows + jnp.arange(rows, dtype=jnp.int32)
    key_index = jnp.arange(total_len, dtype=jnp.int32)
    return (seg_query[:, None] == seg_whole[None, :]) & (query_index[:, None] >= key_index[None, :])


def raw_scores(query, key_whole, allowed):
    keys_split = key_whole.reshape(key_whole.shape[0], HEADS, HEAD_DIM)
    scores = jnp.einsum(
        "qhd,khd->hqk", query, keys_split, preferred_element_type=jnp.float32
    ) * HEAD_DIM ** (-0.5)
    return jnp.where(allowed[None], scores, -1000000000.0)


def layer_forward(resid_low, weights, seg_whole, positions_row, place):
    (
        attention_gain,
        attention_bias,
        joint_weight,
        joint_bias,
        output_weight,
        output_bias,
        feed_gain,
        feed_bias,
        up_weight,
        up_bias,
        down_weight,
        down_bias,
    ) = weights
    rows = resid_low.shape[0]
    resid = resid_low.astype(jnp.float32)
    attn_in, normed_one, scale_one = norm_parts(
        resid, attention_gain.astype(jnp.float32), attention_bias.astype(jnp.float32)
    )
    attn_low = attn_in.astype(jnp.bfloat16)
    joint = jnp.dot(attn_low, joint_weight, preferred_element_type=jnp.float32) + joint_bias.astype(
        jnp.float32
    )
    half = ROT // 2
    rates = 10000.0 ** (-2.0 * jnp.arange(half, dtype=jnp.float32) / ROT)
    angle = positions_row.astype(jnp.float32)[:, None, None] * rates
    cosine = jnp.cos(angle)
    sine = jnp.sin(angle)
    query = turn_heads(joint[:, :D].reshape(rows, HEADS, HEAD_DIM), cosine, sine, 1.0).astype(
        jnp.bfloat16
    )
    keys = (
        turn_heads(joint[:, D : 2 * D].reshape(rows, HEADS, HEAD_DIM), cosine, sine, 1.0)
        .astype(jnp.bfloat16)
        .reshape(rows, D)
    )
    values = joint[:, 2 * D :].astype(jnp.bfloat16)
    key_whole, value_whole = (
        lax.all_gather(keys, "ctx", axis=0, tiled=True),
        lax.all_gather(values, "ctx", axis=0, tiled=True),
    )
    total_len = key_whole.shape[0]
    scores = raw_scores(query, key_whole, allowed_mask(seg_whole, place, rows))
    top = jnp.max(scores, -1, keepdims=True)
    lse = top + jnp.log(jnp.sum(jnp.exp(scores - top), -1, keepdims=True))
    probs_low = jnp.exp(scores - lse).astype(jnp.bfloat16)
    context = jnp.einsum(
        "hqk,khd->qhd",
        probs_low,
        value_whole.reshape(total_len, HEADS, HEAD_DIM),
        preferred_element_type=jnp.float32,
    )
    context_low = context.reshape(rows, D).astype(jnp.bfloat16)
    attended = jnp.dot(
        context_low, output_weight, preferred_element_type=jnp.float32
    ) + output_bias.astype(jnp.float32)
    feed_in, normed_two, scale_two = norm_parts(
        resid, feed_gain.astype(jnp.float32), feed_bias.astype(jnp.float32)
    )
    feed_low = feed_in.astype(jnp.bfloat16)
    upward = jnp.dot(feed_low, up_weight, preferred_element_type=jnp.float32) + up_bias.astype(
        jnp.float32
    )
    active = gelu_value(upward).astype(jnp.bfloat16)
    result = (
        resid
        + attended
        + jnp.dot(active, down_weight, preferred_element_type=jnp.float32)
        + down_bias.astype(jnp.float32)
    ).astype(jnp.bfloat16)
    return (
        result,
        (
            attn_low,
            normed_one,
            scale_one,
            query,
            key_whole,
            value_whole,
            lse,
            context_low,
            feed_low,
            normed_two,
            scale_two,
            upward,
            active,
            cosine,
            sine,
        ),
    )


def layer_backward(grad_low, weights, saved, seg_whole, place):
    (
        attention_gain,
        attention_bias,
        joint_weight,
        joint_bias,
        output_weight,
        output_bias,
        feed_gain,
        feed_bias,
        up_weight,
        up_bias,
        down_weight,
        down_bias,
    ) = weights
    (
        attn_low,
        normed_one,
        scale_one,
        query,
        key_whole,
        value_whole,
        lse,
        context_low,
        feed_low,
        normed_two,
        scale_two,
        upward,
        active,
        cosine,
        sine,
    ) = saved
    rows = grad_low.shape[0]
    total_len = key_whole.shape[0]
    grad_res = grad_low.astype(jnp.float32)
    grad_up = (back_dot(grad_low, down_weight) * gelu_slope(upward)).astype(jnp.bfloat16)
    grad_feed = back_dot(grad_up, up_weight)
    grad_context = (
        back_dot(grad_low, output_weight).astype(jnp.bfloat16).reshape(rows, HEADS, HEAD_DIM)
    )
    keys_split = key_whole.reshape(total_len, HEADS, HEAD_DIM)
    values_split = value_whole.reshape(total_len, HEADS, HEAD_DIM)
    probs = jnp.exp(raw_scores(query, key_whole, allowed_mask(seg_whole, place, rows)) - lse)
    grad_probs = jnp.einsum(
        "qhd,khd->hqk", grad_context, values_split, preferred_element_type=jnp.float32
    )
    grad_scores = (probs * (grad_probs - jnp.sum(probs * grad_probs, -1, keepdims=True))).astype(
        jnp.bfloat16
    )
    factor = HEAD_DIM ** (-0.5)
    grad_query = (
        jnp.einsum("hqk,khd->qhd", grad_scores, keys_split, preferred_element_type=jnp.float32)
        * factor
    )
    keys_part = (
        jnp.einsum("hqk,qhd->khd", grad_scores, query, preferred_element_type=jnp.float32) * factor
    ).reshape(total_len, D)
    values_part = jnp.einsum(
        "hqk,qhd->khd", probs.astype(jnp.bfloat16), grad_context, preferred_element_type=jnp.float32
    ).reshape(total_len, D)
    grad_keys, grad_values = (
        lax.psum_scatter(
            keys_part.astype(jnp.bfloat16), "ctx", scatter_dimension=0, tiled=True
        ).astype(jnp.float32),
        lax.psum_scatter(
            values_part.astype(jnp.bfloat16), "ctx", scatter_dimension=0, tiled=True
        ).astype(jnp.float32),
    )
    grad_query = turn_heads(grad_query, cosine, sine, -1.0).reshape(rows, D)
    grad_keys = turn_heads(grad_keys.reshape(rows, HEADS, HEAD_DIM), cosine, sine, -1.0).reshape(
        rows, D
    )
    grad_joint = jnp.concatenate([grad_query, grad_keys, grad_values], -1).astype(jnp.bfloat16)
    grad_attn = back_dot(grad_joint, joint_weight)
    grad_in = (
        grad_res
        + norm_back(grad_attn, normed_one, scale_one, attention_gain)
        + norm_back(grad_feed, normed_two, scale_two, feed_gain)
    )
    stats = (
        jnp.sum(grad_attn * normed_one, 0),
        jnp.sum(grad_attn, 0),
        jnp.sum(grad_feed * normed_two, 0),
        jnp.sum(grad_feed, 0),
    )
    return (grad_in.astype(jnp.bfloat16), (grad_up, grad_joint), stats)


def put_slot(store, fresh, slot, valid, count):
    if store is None:
        store = tuple((jnp.zeros((count,) + item.shape, item.dtype) for item in fresh))
    return tuple(
        (
            lax.dynamic_update_index_in_dim(
                held,
                jnp.where(valid, item, lax.dynamic_index_in_dim(held, slot, 0, False)),
                slot,
                0,
            )
            for held, item in zip(store, fresh)
        )
    )


def attention_terms(attn_low, context_low, grad_low, grad_joint, gain_grad, bias_grad):
    return (
        gain_grad,
        bias_grad,
        contract(attn_low, grad_joint),
        jnp.sum(grad_joint.astype(jnp.float32), 0),
        contract(context_low, grad_low),
        jnp.sum(grad_low.astype(jnp.float32), 0),
    )


def feed_terms(feed_low, active, grad_low, grad_up, gain_grad, bias_grad):
    return (
        gain_grad,
        bias_grad,
        contract(feed_low, grad_up),
        jnp.sum(grad_up.astype(jnp.float32), 0),
        contract(active, grad_low),
        jnp.sum(grad_low.astype(jnp.float32), 0),
    )


def flatten(array):
    return array.reshape((-1,) + array.shape[2:])


def shards(
    inputs,
    cotangent,
    segments,
    positions,
    attention_gain,
    attention_bias,
    joint_weight,
    joint_bias,
    output_weight,
    output_bias,
    feed_gain,
    feed_bias,
    up_weight,
    up_bias,
    down_weight,
    down_bias,
):
    weights = (
        lax.all_gather(attention_gain[0], "fsdp", axis=0, tiled=True),
        lax.all_gather(attention_bias[0], "fsdp", axis=0, tiled=True),
        lax.all_gather(joint_weight[0], "fsdp", axis=0, tiled=True),
        lax.all_gather(joint_bias[0], "fsdp", axis=0, tiled=True),
        lax.all_gather(output_weight[0], "fsdp", axis=0, tiled=True),
        lax.all_gather(output_bias[0], "fsdp", axis=0, tiled=True),
        lax.all_gather(feed_gain[0], "fsdp", axis=0, tiled=True),
        lax.all_gather(feed_bias[0], "fsdp", axis=0, tiled=True),
        lax.all_gather(up_weight[0], "fsdp", axis=0, tiled=True),
        lax.all_gather(up_bias[0], "fsdp", axis=0, tiled=True),
        lax.all_gather(down_weight[0], "fsdp", axis=0, tiled=True),
        lax.all_gather(down_bias[0], "fsdp", axis=0, tiled=True),
    )
    section_index = lax.axis_index("section")
    sections = lax.axis_size("section")
    place = lax.axis_index("ctx")
    count = inputs.shape[0]
    rounds = count + sections - 1
    seg_rows = segments[:, 0]
    pos_rows = positions[:, 0]
    received = jnp.zeros(inputs.shape[2:], jnp.bfloat16)
    store = None
    for turn in range(rounds):
        lag = turn - section_index
        slot = jnp.clip(lag, 0, count - 1)
        valid = (lag >= 0) & (lag < count)
        layer_in = jnp.where(section_index == 0, inputs[min(turn, count - 1), 0], received)
        seg_whole = lax.dynamic_index_in_dim(seg_rows, slot, 0, False)
        positions_row = lax.dynamic_index_in_dim(pos_rows, slot, 0, False)
        result, saved = layer_forward(layer_in, weights, seg_whole, positions_row, place)
        store = put_slot(store, (result,) + saved, slot, valid, count)
        if turn + 1 < rounds:
            received = from_behind(result, "section", 1)
    outputs = store[0]
    kept = store[1:]
    back_in = jnp.zeros(inputs.shape[2:], jnp.bfloat16)
    grads_store = None
    for turn in range(rounds):
        lag = turn - (sections - 1 - section_index)
        slot = jnp.clip(lag, 0, count - 1)
        valid = (lag >= 0) & (lag < count)
        grad_low = jnp.where(
            section_index == sections - 1, cotangent[min(turn, count - 1), 0], back_in
        )
        saved = tuple((lax.dynamic_index_in_dim(item, slot, 0, False) for item in kept))
        seg_whole = lax.dynamic_index_in_dim(seg_rows, slot, 0, False)
        grad_in, paired, stats = layer_backward(grad_low, weights, saved, seg_whole, place)
        grads_store = put_slot(
            grads_store, (grad_in, grad_low) + paired + stats, slot, valid, count
        )
        if turn + 1 < rounds:
            back_in = from_behind(grad_in, "section", -1)
    attn_low, context_low, feed_low, active = (kept[0], kept[7], kept[8], kept[12])
    grad_low_all, grad_up_all, grad_joint_all = (grads_store[1], grads_store[2], grads_store[3])
    stats_all = grads_store[4:]
    parts = attention_terms(
        flatten(attn_low),
        flatten(context_low),
        flatten(grad_low_all),
        flatten(grad_joint_all),
        jnp.sum(stats_all[0], 0),
        jnp.sum(stats_all[1], 0),
    ) + feed_terms(
        flatten(feed_low),
        flatten(active),
        flatten(grad_low_all),
        flatten(grad_up_all),
        jnp.sum(stats_all[2], 0),
        jnp.sum(stats_all[3], 0),
    )
    shares = (
        lax.psum_scatter(
            parts[0].astype(jnp.bfloat16), "fsdp", scatter_dimension=0, tiled=True
        ).astype(jnp.float32),
        lax.psum_scatter(
            parts[1].astype(jnp.bfloat16), "fsdp", scatter_dimension=0, tiled=True
        ).astype(jnp.float32),
        lax.psum_scatter(
            parts[2].astype(jnp.bfloat16), "fsdp", scatter_dimension=0, tiled=True
        ).astype(jnp.float32),
        lax.psum_scatter(
            parts[3].astype(jnp.bfloat16), "fsdp", scatter_dimension=0, tiled=True
        ).astype(jnp.float32),
        lax.psum_scatter(
            parts[4].astype(jnp.bfloat16), "fsdp", scatter_dimension=0, tiled=True
        ).astype(jnp.float32),
        lax.psum_scatter(
            parts[5].astype(jnp.bfloat16), "fsdp", scatter_dimension=0, tiled=True
        ).astype(jnp.float32),
        lax.psum_scatter(
            parts[6].astype(jnp.bfloat16), "fsdp", scatter_dimension=0, tiled=True
        ).astype(jnp.float32),
        lax.psum_scatter(
            parts[7].astype(jnp.bfloat16), "fsdp", scatter_dimension=0, tiled=True
        ).astype(jnp.float32),
        lax.psum_scatter(
            parts[8].astype(jnp.bfloat16), "fsdp", scatter_dimension=0, tiled=True
        ).astype(jnp.float32),
        lax.psum_scatter(
            parts[9].astype(jnp.bfloat16), "fsdp", scatter_dimension=0, tiled=True
        ).astype(jnp.float32),
        lax.psum_scatter(
            parts[10].astype(jnp.bfloat16), "fsdp", scatter_dimension=0, tiled=True
        ).astype(jnp.float32),
        lax.psum_scatter(
            parts[11].astype(jnp.bfloat16), "fsdp", scatter_dimension=0, tiled=True
        ).astype(jnp.float32),
    )
    totals = (
        lax.psum(shares[0].astype(jnp.bfloat16), "ctx").astype(jnp.float32),
        lax.psum(shares[1].astype(jnp.bfloat16), "ctx").astype(jnp.float32),
        lax.psum(shares[2].astype(jnp.bfloat16), "ctx").astype(jnp.float32),
        lax.psum(shares[3].astype(jnp.bfloat16), "ctx").astype(jnp.float32),
        lax.psum(shares[4].astype(jnp.bfloat16), "ctx").astype(jnp.float32),
        lax.psum(shares[5].astype(jnp.bfloat16), "ctx").astype(jnp.float32),
        lax.psum(shares[6].astype(jnp.bfloat16), "ctx").astype(jnp.float32),
        lax.psum(shares[7].astype(jnp.bfloat16), "ctx").astype(jnp.float32),
        lax.psum(shares[8].astype(jnp.bfloat16), "ctx").astype(jnp.float32),
        lax.psum(shares[9].astype(jnp.bfloat16), "ctx").astype(jnp.float32),
        lax.psum(shares[10].astype(jnp.bfloat16), "ctx").astype(jnp.float32),
        lax.psum(shares[11].astype(jnp.bfloat16), "ctx").astype(jnp.float32),
    )
    section_out = outputs.reshape((1, count, 1) + outputs.shape[1:])
    input_grad = grads_store[0].reshape((1, count, 1) + grads_store[0].shape[1:])
    return (
        section_out,
        input_grad,
        totals[0][None],
        totals[1][None],
        totals[2][None],
        totals[3][None],
        totals[4][None],
        totals[5][None],
        totals[6][None],
        totals[7][None],
        totals[8][None],
        totals[9][None],
        totals[10][None],
        totals[11][None],
    )


def solution(mesh):
    placed = (
        P(None, "fsdp", "ctx", None),
        P(None, "fsdp", "ctx", None),
        P(None, "fsdp", None),
        P(None, "fsdp", "ctx"),
        P("section", "fsdp"),
        P("section", "fsdp"),
        P("section", "fsdp", None),
        P("section", "fsdp"),
        P("section", "fsdp", None),
        P("section", "fsdp"),
        P("section", "fsdp"),
        P("section", "fsdp"),
        P("section", "fsdp", None),
        P("section", "fsdp"),
        P("section", "fsdp", None),
        P("section", "fsdp"),
    )
    return jax.shard_map(
        shards,
        mesh=mesh,
        in_specs=placed,
        out_specs=(
            P("section", None, "fsdp", "ctx", None),
            P("section", None, "fsdp", "ctx", None),
            P("section", "fsdp"),
            P("section", "fsdp"),
            P("section", "fsdp", None),
            P("section", "fsdp"),
            P("section", "fsdp", None),
            P("section", "fsdp"),
            P("section", "fsdp"),
            P("section", "fsdp"),
            P("section", "fsdp", None),
            P("section", "fsdp"),
            P("section", "fsdp", None),
            P("section", "fsdp"),
        ),
        check_vma=False,
    )
```

profile of v0, /device:TPU:0, one launch (start us, length us, event | category | flops | bytes accessed | tf_op | source)
XLA Modules:
  0.0 977.8 jit_solution(14538432949254576603)
XLA Ops:
  18.6 129.3 %all-reduce.15 = (bf16[1024]{0:T(1024)(128)(2,1)S(1)}, bf16[1024]{0:T(1024)(128)(2,1)S(1)}, bf16[3072]{0:T(1024)(128)(2,1)S(1)}, bf16[1024]{0:T(1024)(128)(2,1)S...) all-reduce(bf16[1024]{0:T(1024)(128)(2,1)S(1)} %dynamic-update-slic, ...), channel_id=9, replica_groups=mesh['section'=2,'ctx'=2,'fsdp'=32] {'fsdp'}, use_global_device_ids=true, to_apply=%add.5 | all-reduce | flops 9216 | bytes 36864
  147.9 17.5 %all-gather.9 = bf16[1,4096]{1,0:T(2,128)(2,1)S(1)} all-gather(bf16[1,128]{1,0:T(2,128)(2,1)} %param.29), channel_id=11, replica_groups=mesh['section'=2,'ctx'=2,'fsdp'=32] {'fsdp'}, dimensions={1}, use_global_device_ids=true | all-gather | bytes 8448 | tf_op jit(solution)/shard_map/all_gather | solution.py:342
  175.2 2.4 fusion.156
  178.4 3.9 fusion.63
  182.4 9.2 all_gather.58
  198.1 8.5 all_gather.59
  214.8 4.8 bitcast_dynamic-update-slice_fusion.2
  223.3 3.2 constant_dynamic-slice_fusion.36
  226.4 5.1 fusion.10
  233.7 5.2 collective-permute-start
  241.6 2.3 copy.272
  247.0 3.9 fusion.66
  258.1 8.4 all_gather.68
  275.2 8.2 all_gather.69
  285.4 6.8 bitcast_dynamic-update-slice_fusion.1
  292.3 3.3 constant_dynamic-slice_fusion.35
  301.2 3.0 collective-permute-start.1
  317.8 8.0 all_gather.70
  332.4 8.4 all_gather.71
  342.9 2.6 bitcast_dynamic-update-slice_fusion.3
  345.5 2.6 constant_dynamic-slice_fusion.20
  364.8 2.8 convolution_convert_fusion.2
  375.5 7.6 bitcast_dynamic-update-slice_fusion
  383.2 8.0 fusion.60
  401.9 2.8 reduce-scatter.17.cloned.1.call-done
  404.7 5.3 fusion.28
  410.0 6.6 fusion.278
  426.0 4.4 collective-permute-done.2
  445.6 2.8 convolution_convert_fusion.1
  454.1 8.2 fusion.57
  473.0 7.6 reduce-scatter.19.cloned.1.call-done
  480.5 5.3 fusion.26
  485.9 7.1 fusion.267
  501.0 5.0 collective-permute-done.3
  528.2 2.8 convolution_convert_fusion
  537.0 3.0 convolution_convert_fusion.3
  543.6 3.3 bitcast_convert_fusion.3
  561.3 2.4 fusion.200
  572.2 2.5 fusion.201
  574.7 5.9 bitcast_convert_fusion.2
  581.9 2.3 copy.264
  587.9 2.3 copy.265
  590.2 2.7 fusion.177
  593.0 2.3 copy.266
  599.8 2.3 copy.267
  602.1 7.3 fusion.54
  611.5 2.3 copy.268
  613.8 2.3 constant_dynamic-update-slice_fusion.2
  616.1 7.5 bitcast_convert_fusion.1
  623.6 2.3 copy.273
  625.9 2.3 constant_dynamic-update-slice_fusion
  630.5 2.3 copy.274
  632.8 3.9 fusion.174
  638.9 2.3 constant_dynamic-update-slice_fusion.6
  641.3 6.2 bitcast_convert_fusion
  650.9 5.1 fusion.6
  660.6 2.3 reduce_sum.490
  663.2 5.3 fusion.24
  668.5 6.9 fusion.256
  677.6 128.0 %all-reduce.14 = (bf16[1024]{0:T(1024)(128)(2,1)S(1)}, bf16[1024]{0:T(1024)(128)(2,1)S(1)}, bf16[3072]{0:T(1024)(128)(2,1)S(1)}, bf16[1024]{0:T(1024)(128)(2,1)S...) all-reduce(bf16[1024]{0:T(1024)(128)(2,1)S(1)} %reduce_sum.469, ...), channel_id=20, replica_groups=mesh['section'=2,'ctx'=2,'fsdp'=32] {'fsdp'}, use_global_device_ids=true, to_apply=%region_37.38.clone | all-reduce | flops 12288 | bytes 49152
  806.1 18.3 %reduce-scatter.27.cloned.1.call-done = bf16[32,4096]{1,0:T(8,128)(2,1)} async-done(((bf16[1024,4096]{1,0:T(8,128)(2,1)}), bf16[32,4096]{1,0:T(8,128)(2,1)}) %reduce-scatter.27.cloned.1.call-update) | async-done | bytes 262160 | tf_op jit(solution)/shard_map/reduce_scatter | solution.py:428
  824.4 95.6 %reduce-scatter.29.cloned.1.call-done = bf16[128,1024]{1,0:T(8,128)(2,1)} async-done(((bf16[4096,1024]{1,0:T(8,128)(2,1)}), bf16[128,1024]{1,0:T(8,128)(2,1)}) %reduce-scatter.29.cloned.1.call-update) | async-done | bytes 262160 | tf_op jit(solution)/shard_map/reduce_scatter | solution.py:434
  920.1 4.9 all-reduce.16
  929.4 34.3 %all-reduce.20.cloned.1.call-done = (bf16[1,32,3072]{2,1,0:T(8,128)(2,1)}, bf16[1,32,1024]{2,1,0:T(8,128)(2,1)}, bf16[1,32,4096]{2,1,0:T(8,128)(2,1)}, bf16[1,128,1024]{2,1,0:T(8,128)(2,1)}) async-done(((bf16[1,32,3072]{2,1,0:T(8,128)(2,1)}, bf16[1,32,1024]{2,1,0:T(8,128)(2,1)}, bf16[1,32,4096]{2,1,0:T(8,128)(2,1)}, bf16[1,128,1024]{2,1,0:T(8,128)(2,1)}), (bf16[1,32,3072]{2,1,0:T(8,128)(2,1)}, ...) | async-done | bytes 786448 | tf_op jit(solution)/shard_map/psum | solution.py:444
  (604 shorter events, 266.7 us)
Async XLA Ops:
  7.2 164.3 %copy-start.10 = (bf16[2,1,128,1024]{3,2,1,0:T(8,128)(2,1)S(1)}, bf16[2,1,128,1024]{3,2,1,0:T(8,128)(2,1)}, u32[]{:S(2)}) copy-start(bf16[2,1,128,1024]{3,2,1,0:T(8,128)(2,1)} %param.16) | copy-start | bytes 1572868
  7.2 168.0 %all-gather.19.cloned.1.call-start = ((), (), s32[]{:S(2)}) async-start(), calls=%async_computation.18 | async-start | bytes 2162688 | tf_op jit(solution)/shard_map/all_gather | solution.py:337
  7.9 170.5 %all-gather.17.cloned.1.call-start = ((), (), s32[]{:S(2)}) async-start(), calls=%async_computation.17 | async-start | bytes 6488064 | tf_op jit(solution)/shard_map/all_gather | solution.py:335
  8.7 205.6 %all-gather.21.cloned.1.call-start = ((), (), s32[]{:S(2)}) async-start(), calls=%async_computation.19 | async-start | bytes 8650752 | tf_op jit(solution)/shard_map/all_gather | solution.py:341
  9.4 217.0 %all-gather.23.cloned.1.call-start = ((), (), s32[]{:S(2)}) async-start(), calls=%async_computation.20 | async-start | bytes 8650752 | tf_op jit(solution)/shard_map/all_gather | solution.py:343
  10.0 165.2 %copy-start.58 = (bf16[2,1,128,1024]{3,2,1,0:T(8,128)(2,1)S(1)}, bf16[2,1,128,1024]{3,2,1,0:T(8,128)(2,1)}, u32[]{:S(2)}) copy-start(bf16[2,1,128,1024]{3,2,1,0:T(8,128)(2,1)} %param.17) | copy-start | bytes 1572868
  10.0 381.2 %reduce-scatter.31.cloned.1.call-start = ((), (), s32[]{:S(2)}) async-start(), calls=%async_computation.21 | async-start | bytes 786432
  171.3 43.5 %copy-start.99 = (f32[128]{0:T(128)}, f32[128]{0:T(128)S(1)}, u32[]{:S(2)}) copy-start(f32[128]{0:T(128)S(1)} %add_rsqrt_fusion.2) | copy-start | bytes 1540
  226.4 5.2 copy-start
  226.4 5.2 copy-start.11
  231.6 7.5 copy-start.50
  233.7 11.9 %collective-permute-start = (bf16[128,1024]{1,0:T(8,128)(2,1)}, bf16[128,1024]{1,0:T(8,128)(2,1)}, u32[]{:S(2)}, u32[]{:S(2)}) collective-permute-start(bf16[128,1024]{1,0:T(8,128)(2,1)} %get-tuple-element.253), channel_id=1, source_target_pairs={{0,64},{1,65},{2,66},{3,67},{4,68},{5,69},{6,70},{7,71},{8,72},{9,... | collective-permute-start | bytes 786440 | tf_op jit(solution)/shard_map/ppermute | solution.py:20
  246.7 57.5 %copy-start.97 = (f32[128]{0:T(128)}, f32[128]{0:T(128)S(1)}, u32[]{:S(2)}) copy-start(f32[128]{0:T(128)S(1)} %broadcast_multiply_fusion.13) | copy-start | bytes 1540
  247.0 57.2 %copy-start.101 = (f32[128]{0:T(128)}, f32[128]{0:T(128)S(1)}, u32[]{:S(2)}) copy-start(f32[128]{0:T(128)S(1)} %add_rsqrt_fusion.1) | copy-start | bytes 1540
  285.4 10.1 %copy-start.53 = (bf16[1,128,4096]{2,1,0:T(8,128)(2,1)S(1)}, bf16[1,128,4096]{2,1,0:T(8,128)(2,1)}, u32[]{:S(2)}) copy-start(bf16[1,128,4096]{2,1,0:T(8,128)(2,1)} %copy.272) | copy-start | bytes 3145732
  292.3 6.8 slice-start
  298.5 10.9 %slice-start.2 = ((s8[6291456]{0:T(1024)(128)(4,1)}), s8[4194304]{0:T(1024)(128)(4,1)S(1)}, s32[]{:S(2)}) async-start(s8[6291456]{0:T(1024)(128)(4,1)} %bitcast.774), calls=%async_computation.27 | async-start | bytes 8388608
  299.1 10.3 %slice-start.3 = ((s8[6291456]{0:T(1024)(128)(4,1)}), s8[2097152]{0:T(1024)(128)(4,1)S(1)}, s32[]{:S(2)}) async-start(s8[6291456]{0:T(1024)(128)(4,1)} %bitcast.774), calls=%async_computation.28 | async-start | bytes 4194304
  301.2 9.4 copy-start.44
  301.2 7.7 collective-permute-start.1
  312.4 16.5 %copy-start.112 = (f32[128,8]{0,1:T(8,128)S(1)}, f32[128,8]{0,1:T(8,128)}, u32[]{:S(2)}) copy-start(f32[128,8]{0,1:T(8,128)} %get-tuple-element.229) | copy-start | bytes 12292
  312.4 16.5 %copy-start.113 = (f32[128,8]{0,1:T(8,128)S(1)}, f32[128,8]{0,1:T(8,128)}, u32[]{:S(2)}) copy-start(f32[128,8]{0,1:T(8,128)} %get-tuple-element.230) | copy-start | bytes 12292
  364.7 39.9 %reduce-scatter.17.cloned.1.call-start = ((), (), s32[]{:S(2)}) async-start(), calls=%async_computation.10 | async-start | bytes 786432 | tf_op jit(solution)/shard_map/reduce_scatter | solution.py:248
  367.6 4.9 copy-start.116
  367.6 7.4 copy-start.104
  369.7 5.3 copy-start.4
  369.7 5.3 copy-start.71
  375.3 87.0 %reduce-scatter.33.cloned.1.call-start = ((), (), s32[]{:S(2)}) async-start(), calls=%async_computation.22 | async-start | bytes 786432
  375.5 7.7 copy-start.59
  383.1 11.8 %copy-start.109 = (f32[128,8]{0,1:T(8,128)S(1)}, f32[128,8]{0,1:T(8,128)}, u32[]{:S(2)}) copy-start(f32[128,8]{0,1:T(8,128)} %get-tuple-element.196) | copy-start | bytes 12292
  383.1 11.8 %copy-start.110 = (f32[128,8]{0,1:T(8,128)S(1)}, f32[128,8]{0,1:T(8,128)}, u32[]{:S(2)}) copy-start(f32[128,8]{0,1:T(8,128)} %get-tuple-element.281) | copy-start | bytes 12292
  404.7 5.3 copy-start.54
  410.0 7.5 copy-start.60
  418.7 11.8 %collective-permute-start.2 = (bf16[128,1024]{1,0:T(8,128)(2,1)}, bf16[128,1024]{1,0:T(8,128)(2,1)}, u32[]{:S(2)}, u32[]{:S(2)}) collective-permute-start(bf16[128,1024]{1,0:T(8,128)(2,1)} %get-tuple-element.138), channel_id=1, source_target_pairs={{64,0},{65,1},{66,2},{67,3},{68,4},{69,5},{70,6},{71,7},{72,8},{73... | collective-permute-start | bytes 786440 | tf_op jit(solution)/shard_map/ppermute | solution.py:20
  443.9 36.6 %reduce-scatter.19.cloned.1.call-start = ((), (), s32[]{:S(2)}) async-start(), calls=%async_computation.11 | async-start | bytes 786432 | tf_op jit(solution)/shard_map/reduce_scatter | solution.py:248
  454.0 12.0 %copy-start.107 = (f32[128,8]{0,1:T(8,128)S(1)}, f32[128,8]{0,1:T(8,128)}, u32[]{:S(2)}) copy-start(f32[128,8]{0,1:T(8,128)} %get-tuple-element.195) | copy-start | bytes 12292
  454.0 12.0 %copy-start.108 = (f32[128,8]{0,1:T(8,128)S(1)}, f32[128,8]{0,1:T(8,128)}, u32[]{:S(2)}) copy-start(f32[128,8]{0,1:T(8,128)} %get-tuple-element.282) | copy-start | bytes 12292
  454.0 111.7 %reduce-scatter.35.cloned.1.call-start = ((), (), s32[]{:S(2)}) async-start(), calls=%async_computation.23 | async-start | bytes 786432
  480.5 5.3 copy-start.55
  485.9 7.2 copy-start.62
  485.9 7.2 copy-start.80
  485.9 7.2 copy-start.114
  494.2 11.8 %collective-permute-start.3 = (bf16[128,1024]{1,0:T(8,128)(2,1)}, bf16[128,1024]{1,0:T(8,128)(2,1)}, u32[]{:S(2)}, u32[]{:S(2)}) collective-permute-start(bf16[128,1024]{1,0:T(8,128)(2,1)} %get-tuple-element.136), channel_id=1, source_target_pairs={{64,0},{65,1},{66,2},{67,3},{68,4},{69,5},{70,6},{71,7},{72,8},{73... | collective-permute-start | bytes 786440 | tf_op jit(solution)/shard_map/ppermute | solution.py:20
  516.1 4.1 copy-start.100
  519.3 52.9 %reduce-scatter.21.cloned.1.call-start = ((), (), s32[]{:S(2)}) async-start(), calls=%async_computation.12 | async-start | bytes 786432 | tf_op jit(solution)/shard_map/reduce_scatter | solution.py:248
  531.0 6.0 copy-start.94
  533.1 273.0 %reduce-scatter.25.cloned.1.call-start = ((), (), s32[]{:S(2)}) async-start(), calls=%async_computation.14 | async-start | bytes 2162688 | tf_op jit(solution)/shard_map/reduce_scatter | solution.py:416
  546.9 259.2 %reduce-scatter.23.cloned.1.call-start = ((), (), s32[]{:S(2)}) async-start(), calls=%async_computation.13 | async-start | bytes 6488064 | tf_op jit(solution)/shard_map/reduce_scatter | solution.py:410
  547.0 4.3 copy-start.5
  550.3 4.7 copy-start.63
  580.6 243.8 %reduce-scatter.27.cloned.1.call-start = ((), (), s32[]{:S(2)}) async-start(), calls=%async_computation.15 | async-start | bytes 8650752 | tf_op jit(solution)/shard_map/reduce_scatter | solution.py:428
  602.1 8.3 copy-start.52
  623.6 296.4 %reduce-scatter.29.cloned.1.call-start = ((), (), s32[]{:S(2)}) async-start(), calls=%async_computation.16 | async-start | bytes 8650752 | tf_op jit(solution)/shard_map/reduce_scatter | solution.py:434
  647.5 316.2 %all-reduce.20.cloned.1.call-start = ((), (), s32[]{:S(2)}) async-start(), calls=%async_computation.24 | async-start | bytes 1572864 | tf_op jit(solution)/shard_map/psum | solution.py:444
  650.9 5.1 copy-start.6
  650.9 5.1 copy-start.45
  650.9 5.1 copy-start.69
  657.8 5.3 copy-start.65
  658.9 4.3 copy-start.87
  663.2 5.3 copy-start.57
  675.4 252.7 %copy-start.68 = (bf16[128,1024]{1,0:T(8,128)(2,1)S(1)}, bf16[128,1024]{1,0:T(8,128)(2,1)}, u32[]{:S(2)}) copy-start(bf16[128,1024]{1,0:T(8,128)(2,1)} %copy-done.67) | copy-start | bytes 786436
  675.4 252.7 %copy-start.119 = (f32[128]{0:T(128)S(1)}, f32[128]{0:T(128)}, u32[]{:S(2)}) copy-start(f32[128]{0:T(128)} %get-tuple-element.222) | copy-start | bytes 1540
  926.5 44.0 %copy-start.120 = (f32[1,32]{1,0:T(1,128)}, f32[1,32]{1,0:T(1,128)S(1)}, u32[]{:S(2)}) copy-start(f32[1,32]{1,0:T(1,128)S(1)} %broadcast_in_dim.398) | copy-start | bytes 388
  929.4 41.6 %copy-start.83 = (bf16[1,2,1,128,1024]{4,3,2,1,0:T(8,128)(2,1)}, bf16[1,2,1,128,1024]{4,3,2,1,0:T(8,128)(2,1)S(1)}, u32[]{:S(2)}) copy-start(bf16[1,2,1,128,1024]{4,3,2,1,0:T(8,128)(2,1)S(1)} %bitcast_dynamic-update-slice_fusion.16) | copy-start | bytes 1572868
  (80 other events, 161.2 us)
Sparse Core Ops, SparseCore 0:
  10.3 46.1 all-gather.18
  58.8 48.3 all-gather.16
  109.4 51.8 all-gather.20
  163.4 52.3 all-gather.22
  364.9 19.2 reduce-scatter.30
  386.5 18.1 reduce-scatter.16
  444.0 15.8 reduce-scatter.32
  462.4 18.1 reduce-scatter.18
  519.4 15.8 reduce-scatter.34
  537.6 18.0 reduce-scatter.20
  559.3 79.5 reduce-scatter.24
  642.6 85.6 reduce-scatter.22
  732.4 91.9 reduce-scatter.26
  828.0 91.9 reduce-scatter.28
  922.7 41.0 all-reduce.19
where the time goes:
time: 988 us; the launch traced here: 978 us
  blocking collectives  331 us (34%)
  local copies, waits for them, and re-layouts  197 us (20%)
  waiting for transfers between devices  171 us (17%)
  matrix products  163 us (16%)
  other arithmetic  85 us (9%)
  between operations  19.7 us (2%)
  starting transfers between devices  12.2 us (1%)
    unnamed x2, blocking collectives  257 us
    reduce_scatter x1, waiting for transfers between devices, shards(): lax.psum_scatter(parts[10].astype(jnp.bfloat16), 'fsdp', scatter_dimensio...  95.6 us
    dot_general x12, matrix products, back_dot(): lax.dot_general(left, weight, (((1,), (1,)), ((), ())), preferred_element...  65.7 us
    unnamed x274, local copies, waits for them, and re-layouts  36.1 us
    dynamic_slice x23, local copies, waits for them, and re-layouts, put_slot(): lax.dynamic_index_in_dim(held, slot, 0, False)  34.5 us
    psum x1, waiting for transfers between devices, shards(): lax.psum(shares[2].astype(jnp.bfloat16), 'ctx').astype(jnp.float32)  34.3 us
    dynamic_update_slice x36, other arithmetic, put_slot(): lax.dynamic_update_index_in_dim(held, jnp.where(valid, item, lax.dynamic_...  32.8 us
    all_gather x3, blocking collectives, layer_forward(): lax.all_gather(values, 'ctx', axis=0, tiled=True)  25.6 us
  transfers between devices with their start and end apart: 19, of which 7 were waited for; matrix products, arithmetic and copies ran while one was open for 29% of the time, Pallas kernels for 0%

commit v1 on v0

v1 whole, which is shorter than its diff:
```python
import functools
import math

import jax
import jax.numpy as jnp
from jax import lax
from jax.experimental import pallas as pl
from jax.experimental.pallas import tpu as pltpu
from jax.sharding import Mesh
from jax.sharding import PartitionSpec as P

D = 1024
HEAD_DIM = 64
ROT = 16
SEQ = 256
LOCAL = 256
FEED = 1024
HERE = LOCAL // HEAD_DIM
EPSILON = 1e-05
LOW = jnp.bfloat16
FULL = jnp.float32
VMEM = 56 * 1024 * 1024


def shift(block, axis, distance):
    size = lax.axis_size(axis)
    return lax.ppermute(block, axis, [(i, (i + distance) % size) for i in range(size)])


def gather_four(block, axis, dim):
    me = lax.axis_index(axis)
    whole = jnp.zeros(block.shape[:dim] + (4,) + block.shape[dim:], block.dtype)
    parts = [(0, block)] + [(d, shift(block, axis, d)) for d in (1, 3, 2)]
    for distance, part in parts:
        whole = lax.dynamic_update_slice_in_dim(
            whole, jnp.expand_dims(part, dim), (me - distance) % 4, dim
        )
    return whole


def scatter_four(block, axis, dim):
    me = lax.axis_index(axis)

    def quarter(index):
        return lax.dynamic_index_in_dim(block, index % 4, dim, False)

    total = quarter(me).astype(FULL)
    for distance in (1, 3, 2):
        total = total + shift(quarter(me + distance), axis, distance).astype(FULL)
    return total


def in_order(index, own, other, dim):
    return jnp.where(
        index == 0,
        jnp.concatenate([own, other], dim),
        jnp.concatenate([other, own], dim),
    )


def pair(block, axis, dim):
    return in_order(lax.axis_index(axis), block, shift(block, axis, 1), dim)


def dot(left, right):
    return jnp.dot(left, right, preferred_element_type=FULL)


def dot_back(left, right):
    return lax.dot_general(left, right, (((1,), (1,)), ((), ())), preferred_element_type=FULL)


def dot_over(left, right):
    return lax.dot_general(left, right, (((0,), (0,)), ((), ())), preferred_element_type=FULL)


def turn(heads, cosine, sine):
    lane = lax.broadcasted_iota(jnp.int32, heads.shape, 1) % HEAD_DIM
    partner = jnp.where(
        lane < ROT // 2,
        pltpu.roll(heads, LOCAL - ROT // 2, 1),
        pltpu.roll(heads, ROT // 2, 1),
    )
    return heads * cosine + partner * sine


def normalize(hidden):
    centred = hidden - jnp.mean(hidden, -1, keepdims=True)
    scale = lax.rsqrt(jnp.mean(centred * centred, -1, keepdims=True) + EPSILON)
    return centred * scale, scale


def head_lanes(head):
    lane = lax.broadcasted_iota(jnp.int32, (SEQ, LOCAL), 1)
    return lane // HEAD_DIM == head


def allowed_keys(seg_row, seg_col):
    query = lax.broadcasted_iota(jnp.int32, (SEQ, SEQ), 0)
    key = lax.broadcasted_iota(jnp.int32, (SEQ, SEQ), 1)
    return (seg_col == seg_row) & (query >= key)


def forward_kernel(
    keep, hidden, seg_row, seg_col, cosine, sine, params, w_query, w_pair, w_out, w_up, w_down, *out
):
    normed, _ = normalize(hidden[0].astype(FULL))
    first = (normed * params[0:1] + params[1:2]).astype(LOW)
    second = (normed * params[2:3] + params[3:4]).astype(LOW)
    cos = jnp.concatenate([cosine[0]] * 2, 1)
    sin = jnp.concatenate([sine[0]] * 2, 1)
    query = turn(dot(first, w_query[...]) + params[4:5, :LOCAL], cos, sin)
    both = dot(first, w_pair[...]) + params[4:5, LOCAL : 3 * LOCAL]
    keys = turn(both[:, :LOCAL], cos, sin).astype(LOW)
    values = both[:, LOCAL:].astype(LOW)
    allowed = allowed_keys(seg_row[0], seg_col[0])
    context = jnp.zeros((SEQ, LOCAL), FULL)
    lanes = lax.broadcasted_iota(jnp.int32, (SEQ, 128), 1)
    kept_lse = jnp.zeros((SEQ, 128), FULL)
    for head in range(HERE):
        mine = head_lanes(head)
        scores = dot_back(jnp.where(mine, query, 0.0).astype(LOW), keys) * HEAD_DIM**-0.5
        scores = jnp.where(allowed, scores, -1000000000.0)
        top = jnp.max(scores, -1, keepdims=True)
        weight = jnp.exp(scores - top)
        total = jnp.sum(weight, -1, keepdims=True)
        probs = (weight * (1.0 / total)).astype(LOW)
        context = jnp.where(mine, dot(probs, values), context)
        if keep:
            kept_lse = jnp.where(lanes == head, top + jnp.log(total), kept_lse)
    context = context.astype(LOW)
    upward = dot(second, w_up[...]) + params[5:6]
    half = 0.5 * (1.0 + lax.erf(upward * math.sqrt(0.5)))
    active = (upward * half).astype(LOW)
    out[0][0] = (dot(context, w_out[...]) + dot(active, w_down[...])).astype(LOW)
    if keep:
        slope = half + upward * jnp.exp(-0.5 * upward * upward) * math.sqrt(0.5 / math.pi)
        out[1][0] = first
        out[2][0] = second
        out[3][0] = query.astype(LOW)
        out[4][0] = keys
        out[5][0] = values
        out[6][0] = kept_lse
        out[7][0] = context
        out[8][0] = active
        out[9][0] = slope.astype(LOW)


def backward_kernel(
    keep,
    grad,
    hidden,
    seg_row,
    seg_col,
    cosine,
    sine,
    params,
    w_query,
    w_pair,
    w_out,
    w_up,
    w_down,
    query_in,
    keys_in,
    values_in,
    lse_in,
    slope,
    *out,
):
    g = grad[0]
    normed, scale = normalize(hidden[0].astype(FULL))
    up_grad = (dot_back(g, w_down[...]) * slope[0].astype(FULL)).astype(LOW)
    second_grad = dot_back(up_grad, w_up[...])
    context_grad = dot_back(g, w_out[...])
    context_low = context_grad.astype(LOW)
    query = query_in[0]
    keys = keys_in[0]
    values = values_in[0]
    query_full = query.astype(FULL)
    allowed = allowed_keys(seg_row[0], seg_col[0])
    query_grad = jnp.zeros((SEQ, LOCAL), FULL)
    keys_grad = jnp.zeros((SEQ, LOCAL), FULL)
    values_grad = jnp.zeros((SEQ, LOCAL), FULL)
    for head in range(HERE):
        mine = head_lanes(head)
        scores = dot_back(jnp.where(mine, query_full, 0.0).astype(LOW), keys) * HEAD_DIM**-0.5
        scores = jnp.where(allowed, scores, -1000000000.0)
        probs = jnp.exp(scores - lse_in[0][:, head : head + 1])
        probs_grad = dot_back(jnp.where(mine, context_grad, 0.0).astype(LOW), values)
        scores_grad = (
            probs * (probs_grad - jnp.sum(probs * probs_grad, -1, keepdims=True))
        ).astype(LOW)
        query_grad = jnp.where(mine, dot(scores_grad, keys), query_grad)
        keys_grad = jnp.where(mine, dot_over(scores_grad, query), keys_grad)
        values_grad = jnp.where(mine, dot_over(probs.astype(LOW), context_low), values_grad)
    cos = jnp.concatenate([cosine[0]] * 2, 1)
    sin = -jnp.concatenate([sine[0]] * 2, 1)
    query_low = turn(query_grad * HEAD_DIM**-0.5, cos, sin).astype(LOW)
    pair_low = jnp.concatenate(
        [turn(keys_grad * HEAD_DIM**-0.5, cos, sin), values_grad], 1
    ).astype(LOW)
    first_grad = dot_back(query_low, w_query[...]) + dot_back(pair_low, w_pair[...])
    inner = first_grad * params[0:1] + second_grad * params[2:3]
    out[0][0] = (
        scale
        * (
            inner
            - jnp.mean(inner, -1, keepdims=True)
            - normed * jnp.mean(inner * normed, -1, keepdims=True)
        )
    ).astype(LOW)
    if keep:
        out[1][0] = up_grad
        out[2][0] = query_low
        out[3][0] = pair_low
        out[4][0] = jnp.zeros((8, D), FULL)
        for row, item in enumerate(
            (
                first_grad * normed,
                first_grad,
                second_grad * normed,
                second_grad,
                up_grad.astype(FULL),
                g.astype(FULL),
                query_low.astype(FULL),
                pair_low.astype(FULL),
            )
        ):
            out[4][0, row : row + 1, : item.shape[1]] = jnp.sum(item, 0, keepdims=True)


def per_sequence(*shape):
    return pl.BlockSpec((1,) + shape, lambda i: (i,) + (0,) * len(shape))


def resident(*shape):
    return pl.BlockSpec(shape, lambda i: (0,) * len(shape))


LAYER_SPECS = [
    resident(8, D),
    resident(D, LOCAL),
    resident(D, 2 * LOCAL),
    resident(LOCAL, D),
    resident(D, FEED),
    resident(FEED, D),
]
PLACE_SPECS = [
    per_sequence(1, SEQ),
    per_sequence(SEQ, 1),
    per_sequence(SEQ, 128),
    per_sequence(SEQ, 128),
]
SAVED = (
    (D, LOW),
    (D, LOW),
    (LOCAL, LOW),
    (LOCAL, LOW),
    (LOCAL, LOW),
    (128, FULL),
    (LOCAL, LOW),
    (FEED, LOW),
    (FEED, LOW),
)


def forward(hidden, place, layer, keep):
    count = hidden.shape[0]
    widths = ((D, LOW),) + (SAVED if keep else ())
    return pl.pallas_call(
        functools.partial(forward_kernel, keep),
        grid=(count,),
        in_specs=[per_sequence(SEQ, D)] + PLACE_SPECS + LAYER_SPECS,
        out_specs=[per_sequence(SEQ, width) for width, _ in widths],
        out_shape=[jax.ShapeDtypeStruct((count, SEQ, width), kind) for width, kind in widths],
        compiler_params=pltpu.CompilerParams(vmem_limit_bytes=VMEM),
        cost_estimate=pl.CostEstimate(
            flops=count * SEQ * 6 * D * D, bytes_accessed=count * 4 * D * D, transcendentals=0
        ),
        name="layer_forward",
    )(hidden, *place, *layer)


def backward(grad, hidden, place, layer, saved, keep):
    count = hidden.shape[0]
    shapes = [((SEQ, D), LOW)]
    if keep:
        shapes += [
            ((SEQ, FEED), LOW),
            ((SEQ, LOCAL), LOW),
            ((SEQ, 2 * LOCAL), LOW),
            ((8, D), FULL),
        ]
    return pl.pallas_call(
        functools.partial(backward_kernel, keep),
        grid=(count,),
        in_specs=[per_sequence(SEQ, D)] * 2
        + PLACE_SPECS
        + LAYER_SPECS
        + [
            per_sequence(SEQ, LOCAL),
            per_sequence(SEQ, LOCAL),
            per_sequence(SEQ, LOCAL),
            per_sequence(SEQ, 128),
            per_sequence(SEQ, FEED),
        ],
        out_specs=[per_sequence(*shape) for shape, _ in shapes],
        out_shape=[jax.ShapeDtypeStruct((count,) + shape, kind) for shape, kind in shapes],
        compiler_params=pltpu.CompilerParams(vmem_limit_bytes=VMEM),
        cost_estimate=pl.CostEstimate(
            flops=count * SEQ * 6 * D * D, bytes_accessed=count * 4 * D * D, transcendentals=0
        ),
        name="layer_backward",
    )(grad, hidden, *place, *layer, saved[2], saved[3], saved[4], saved[5], saved[8])


SMALL = (32, 32, 96, 32, 32, 32, 128, 32)


def fetch_layer(small, joint_weight, output_weight, up_weight, down_weight):
    c = lax.axis_index("ctx")
    k = lax.axis_index("core")
    quarter = 2 * c + k
    joint_cut = joint_weight.reshape(32, 3, 4, 4, HEAD_DIM)
    joint_parts = [joint_cut[:, :, :, q].reshape(32, 3 * LOCAL) for q in range(4)]
    up_cut = up_weight.reshape(32, 16, 2, 2, HEAD_DIM)
    up_parts = [up_cut[:, :, q % 2, q // 2].reshape(32, FEED) for q in range(4)]

    def columns(index):
        return [lax.select_n(index, *joint_parts), lax.select_n(index, *up_parts)]

    flat = jnp.concatenate(small + (jnp.zeros((512 - sum(SMALL),), LOW),)).reshape(4, 128)
    flat = jnp.concatenate([flat, jnp.zeros((28, 128), LOW)], 0)
    shared = [output_weight, flat]
    own = jnp.concatenate(columns(quarter) + shared, 1)
    other = shift(jnp.concatenate(columns(quarter ^ 1) + shared, 1), "core", 1)
    block = in_order(k, own, other, 0)
    joint, up, out, flat = jnp.split(block, (768, 1792, 2816), 1)
    down = lax.dynamic_slice_in_dim(down_weight, c * 64, 64, 0)
    query = jnp.concatenate([joint[:, :LOCAL], flat], 1)
    mixed = gather_four(jnp.concatenate([out, query], 1), "x", 0)
    keyed = gather_four(joint[:, LOCAL:], "y", 0)
    out = lax.dynamic_index_in_dim(mixed, quarter, 0, False)[:, :D]
    out = gather_four(out, "y", 0).reshape(LOCAL, D)
    query = gather_four(mixed[:, :, D:], "y", 0).reshape(D, LOCAL + 128)
    keyed = gather_four(keyed, "x", 1).reshape(D, 2 * LOCAL)
    up = gather_four(up, "x", 0)
    down = gather_four(down, "y", 0)
    up = gather_four(up, "y", 0).reshape(D, FEED)
    down = gather_four(down, "x", 1).reshape(FEED, D)
    flat = query[:, LOCAL:].reshape(32, 32, 128)[:, :4].reshape(32, 512)
    edges = [sum(SMALL[:i]) for i in range(len(SMALL) + 1)]
    small = [flat[:, a:b].reshape(-1).astype(FULL) for a, b in zip(edges, edges[1:])]
    joint_bias = lax.dynamic_index_in_dim(
        small[2].reshape(3, 4, 4, HEAD_DIM), quarter, 2, False
    ).reshape(-1)
    up_bias = small[6].reshape(16, 2, 2, HEAD_DIM)
    up_bias = lax.dynamic_index_in_dim(
        lax.dynamic_index_in_dim(up_bias, c, 2, False), k, 1, False
    ).reshape(-1)
    params = jnp.stack(
        [
            small[0],
            small[1],
            small[4],
            small[5],
            jnp.pad(joint_bias, (0, D - 3 * LOCAL)),
            up_bias,
            small[3] + small[7],
            jnp.zeros((D,), FULL),
        ]
    )
    return params, query, keyed, out, up, down


def both_quarters(block):
    k = lax.axis_index("core")
    rows = block.astype(LOW).reshape(2, 32, -1)
    own = lax.dynamic_index_in_dim(rows, k, 0)
    other = shift(lax.dynamic_index_in_dim(rows, 1 - k, 0), "core", 1)
    return pair(in_order(k, own, other, 0), "ctx", 0)


def summed_quarters(block):
    k = lax.axis_index("core")
    rows = block.astype(LOW).reshape(2, 32, -1)
    other = shift(lax.dynamic_index_in_dim(rows, 1 - k, 0, False), "core", 1)
    total = (lax.dynamic_index_in_dim(rows, k, 0, False).astype(FULL) + other.astype(FULL)).astype(
        LOW
    )
    return total.astype(FULL) + shift(total, "ctx", 1).astype(FULL)


def chunks(block):
    return block.astype(LOW).reshape(4, 4, 64, -1)


def return_down(term):
    block = scatter_four(chunks(term), "x", 1).astype(LOW)
    block = scatter_four(block, "y", 0).astype(LOW)
    return pair(block, "ctx", 0).astype(FULL)


def return_up(term):
    block = scatter_four(chunks(term), "y", 0).astype(LOW)
    block = both_quarters(scatter_four(block, "x", 0))
    return block.reshape(2, 2, 32, 16, HEAD_DIM).transpose(2, 3, 1, 0, 4).reshape(32, -1).astype(FULL)


def return_out(term):
    quarter = 2 * lax.axis_index("ctx") + lax.axis_index("core")
    block = scatter_four(term.astype(LOW).reshape(4, 64, D), "y", 0).astype(LOW)
    block = jnp.where(jnp.arange(4)[:, None, None] == quarter, block[None], jnp.zeros_like(block[None]))
    return summed_quarters(scatter_four(block, "x", 0))


def return_joint(query_term, pair_term, small_terms):
    block = jnp.concatenate([query_term.astype(LOW), small_terms.astype(LOW)], 1)
    block = scatter_four(chunks(block), "y", 0).astype(LOW)
    other = scatter_four(chunks(pair_term), "x", 1).astype(LOW)
    block = scatter_four(block, "x", 0)
    other = scatter_four(other, "y", 0)
    joint = both_quarters(jnp.concatenate([block[:, :LOCAL], other], 1))
    joint = joint.reshape(4, 32, 3, 4, HEAD_DIM).transpose(1, 2, 3, 0, 4).reshape(32, -1)
    flat = summed_quarters(block[:, LOCAL:])[:4].reshape(-1)
    edges = [sum(SMALL[:i]) for i in range(len(SMALL) + 1)]
    return joint.astype(FULL), [flat[a:b] for a, b in zip(edges, edges[1:])]


def pack_small(sums):
    c = lax.axis_index("ctx")
    k = lax.axis_index("core")
    quarter = 2 * c + k
    joint = jnp.concatenate([sums[6, :LOCAL], sums[7, : 2 * LOCAL]]).reshape(3, 4, 1, HEAD_DIM)
    joint = jnp.where(jnp.arange(4)[:, None] == quarter, joint, 0.0)
    where_up = (jnp.arange(2)[:, None, None] == k) & (jnp.arange(2)[:, None] == c)
    up = jnp.where(where_up, sums[4].reshape(16, 1, 1, HEAD_DIM), 0.0)
    grads = sums[5] * 0.25
    items = (sums[0], sums[1], joint, grads, sums[2], sums[3], up, grads)
    flat = [item.reshape(32, -1) for item in items] + [jnp.zeros((32, 512 - sum(SMALL)), FULL)]
    flat = jnp.concatenate(flat, 1).reshape(32, 4, 128)
    return jnp.pad(flat, ((0, 0), (0, 28), (0, 0))).reshape(D, 128)


def reduce_own(partial):
    c = lax.axis_index("ctx")
    k = lax.axis_index("core")
    other = shift(lax.dynamic_index_in_dim(partial, 1 - k, 0, False), "core", 1)
    total = lax.dynamic_index_in_dim(partial, k, 0, False).astype(FULL) + other.astype(FULL)
    half = total.reshape(2, SEQ // 2, D)
    other = shift(lax.dynamic_index_in_dim(half, 1 - c, 0, False).astype(LOW), "ctx", 1)
    return lax.dynamic_index_in_dim(half, c, 0, False) + other.astype(FULL)


def hand_on(block, start, end):
    c = lax.axis_index("ctx")
    same = lax.ppermute(
        block, ("section", "ctx"), [(2 * start, 2 * end), (2 * start + 1, 2 * end + 1)]
    )
    flip = lax.ppermute(
        block, ("section", "ctx"), [(2 * start, 2 * end + 1), (2 * start + 1, 2 * end)]
    )
    whole = in_order(c, same, flip, 0)
    return pair(whole[None], "core", 0)


def shards(
    inputs,
    cotangent,
    segments,
    positions,
    attention_gain,
    attention_bias,
    joint_weight,
    joint_bias,
    output_weight,
    output_bias,
    feed_gain,
    feed_bias,
    up_weight,
    up_bias,
    down_weight,
    down_bias,
):
    section = lax.axis_index("section")
    count = inputs.shape[0]
    layer = fetch_layer(
        (
            attention_gain[0],
            attention_bias[0],
            joint_bias[0],
            output_bias[0],
            feed_gain[0],
            feed_bias[0],
            up_bias[0],
            down_bias[0],
        ),
        joint_weight[0],
        output_weight[0],
        up_weight[0],
        down_weight[0],
    )
    bias = layer[0][6]
    whole_in = pair(pair(inputs, "ctx", 2), "core", 1)
    whole_grad = pair(pair(cotangent, "ctx", 2), "core", 1)
    seg = pair(segments, "core", 1)
    pos = pair(pair(positions, "ctx", 2), "core", 1)
    lane = jnp.arange(128) % HEAD_DIM
    rates = jnp.where(lane < ROT, 10000.0 ** (-2.0 * (lane % (ROT // 2)).astype(FULL) / ROT), 0.0)
    angle = pos.astype(FULL)[..., None] * rates
    cosine = jnp.cos(angle)
    sine = jnp.sin(angle) * jnp.where(lane < ROT // 2, -1.0, 1.0)
    places = [(seg[m][:, None, :], seg[m][:, :, None], cosine[m], sine[m]) for m in range(count)]
    own_in = inputs[:, 0].astype(FULL)
    hidden = []
    for m in range(count):
        (partial,) = forward(whole_in[m], places[m], layer, False)
        result = (own_in[m] + bias + reduce_own(partial)).astype(LOW)
        hidden.append(jnp.where(section == 0, whole_in[m], hand_on(result, 0, 1)))
    c = lax.axis_index("ctx")
    k = lax.axis_index("core")
    saved = []
    outputs = []
    for m in range(count):
        partial, *kept = forward(hidden[m], places[m], layer, True)
        own = lax.dynamic_index_in_dim(hidden[m], k, 0, False).reshape(2, SEQ // 2, D)
        own = lax.dynamic_index_in_dim(own, c, 0, False).astype(FULL)
        outputs.append((own + bias + reduce_own(partial)).astype(LOW))
        saved.append(kept)
    own_grad = cotangent[:, 0].astype(FULL)
    grads = []
    for m in range(count):
        (partial,) = backward(whole_grad[m], hidden[m], places[m], layer, saved[m], False)
        result = (own_grad[m] + reduce_own(partial)).astype(LOW)
        grads.append(jnp.where(section == 1, whole_grad[m], hand_on(result, 1, 0)))
    grad_all = jnp.concatenate(grads, 0).reshape(-1, D)

    def all_tokens(index):
        return jnp.concatenate([kept[index] for kept in saved], 0).reshape(count * 2 * SEQ, -1)

    down_grad = return_down(dot_over(all_tokens(7), grad_all))
    out_grad = return_out(dot_over(all_tokens(6), grad_all))
    input_grads = []
    terms = []
    for m in range(count):
        partial, *more = backward(grads[m], hidden[m], places[m], layer, saved[m], True)
        own = lax.dynamic_index_in_dim(grads[m], k, 0, False).reshape(2, SEQ // 2, D)
        own = lax.dynamic_index_in_dim(own, c, 0, False).astype(FULL)
        input_grads.append((own + reduce_own(partial)).astype(LOW))
        terms.append(more)

    def all_terms(index):
        return jnp.concatenate([more[index] for more in terms], 0).reshape(count * 2 * SEQ, -1)

    up_grad = return_up(dot_over(all_tokens(1), all_terms(0)))
    sums = sum(jnp.sum(more[3], 0) for more in terms)
    first = all_tokens(0)
    joint_grad, small = return_joint(
        dot_over(first, all_terms(1)), dot_over(first, all_terms(2)), pack_small(sums)
    )
    section_out = jnp.stack(outputs)[None, :, None]
    input_grad = jnp.stack(input_grads)[None, :, None]
    return (
        section_out,
        input_grad,
        small[0][None],
        small[1][None],
        joint_grad[None],
        small[2][None],
        out_grad[None],
        small[3][None],
        small[4][None],
        small[5][None],
        up_grad[None],
        small[6][None],
        down_grad[None],
        small[7][None],
    )


def solution(mesh):
    finer = Mesh(mesh.devices.reshape(2, 2, 4, 4, 2), ("section", "ctx", "y", "x", "core"))
    fsdp = ("y", "x", "core")
    vector = P("section", fsdp)
    matrix = P("section", fsdp, None)
    tokens = P(None, fsdp, "ctx", None)
    kept = P("section", None, fsdp, "ctx", None)
    params = (
        vector,
        vector,
        matrix,
        vector,
        matrix,
        vector,
        vector,
        vector,
        matrix,
        vector,
        matrix,
        vector,
    )
    return jax.shard_map(
        shards,
        mesh=finer,
        in_specs=(tokens, tokens, P(None, fsdp, None), P(None, fsdp, "ctx")) + params,
        out_specs=(kept, kept) + params,
        check_vma=False,
    )
```

time: 988 us -> 526 us (0.53)
  blocking collectives: 331 us -> 0 us
  matrix products: 163 us -> 11.3 us
  local copies, waits for them, and re-layouts: 197 us -> 58.5 us
  starting transfers between devices: 12.2 us -> 119 us
  Pallas kernels: 0 us -> 98.3 us
  other arithmetic: 85 us -> 35.6 us
  waiting for transfers between devices: 171 us -> 190 us
  between operations: 19.7 us -> 3.27 us
    unnamed x2 -> x0, blocking collectives: 257 us -> none
    ppermute x4 -> x102, waiting for transfers between devices: 9.42 us -> 190 us  [the longest x94 151 us: shift(): lax.ppermute(block, axis, [(i, (i + distance) % size) for i in range(size)])]
    dot_general x49 -> x5, matrix products: 163 us -> 11.3 us  [dot_over(): lax.dot_general(left, right, (((0,), (0,)), ((), ())), preferred_element_...]
    reduce_scatter x7 -> x0, waiting for transfers between devices: 124 us -> none  [the longest x1 95.6 us: shards(): lax.psum_scatter(parts[10].astype(jnp.bfloat16), 'fsdp', scatter_dimensio...]
    ppermute x4 -> x102, starting transfers between devices: 11.3 us -> 119 us  [the longest x94 104 us: shift(): lax.ppermute(block, axis, [(i, (i + distance) % size) for i in range(size)])]
    pallas_call x0 -> x8, Pallas kernels: none -> 98.3 us  [the longest x4 54.1 us: backward(): pl.pallas_call(functools.partial(backward_kernel, keep), grid=(count,), i...]
    all_gather x7 -> x0, blocking collectives: 68.3 us -> none  [the longest x3 25.6 us: layer_forward(): lax.all_gather(values, 'ctx', axis=0, tiled=True)]
    dynamic_slice x32 -> x8, local copies, waits for them, and re-layouts: 51.6 us -> 2.65 us  [the longest x1 1.58 us: fetch_layer(): down = lax.dynamic_slice_in_dim(down_weight, c * 64, 64, 0)]
  transfers between devices with their start and end apart: 19 -> 102, of which waited for: 7 -> 50; matrix products, arithmetic and copies ran while one was open for 29% -> 16% of each run, Pallas kernels for 0% -> 9%
where the time goes in v1:
time: 526 us; the launch traced here: 516 us
  waiting for transfers between devices  190 us (36%)
  starting transfers between devices  119 us (23%)
  Pallas kernels  98.3 us (19%)
  local copies, waits for them, and re-layouts  58.5 us (11%)
  other arithmetic  35.6 us (7%)
  matrix products  11.3 us (2%)
    ppermute x94, waiting for transfers between devices, shift(): lax.ppermute(block, axis, [(i, (i + distance) % size) for i in range(size)])  151 us
    ppermute x94, starting transfers between devices, shift(): lax.ppermute(block, axis, [(i, (i + distance) % size) for i in range(size)])  104 us
    pallas_call x4, Pallas kernels, backward(): pl.pallas_call(functools.partial(backward_kernel, keep), grid=(count,), i...  54.1 us
    pallas_call x4, Pallas kernels, forward(): pl.pallas_call(functools.partial(forward_kernel, keep), grid=(count,), in...  44.2 us
    ppermute x4, waiting for transfers between devices, hand_on(): lax.ppermute(block, ('section', 'ctx'), [(2 * start, 2 * end + 1), (2 * s...  38.5 us
    dynamic_update_slice x34, local copies, waits for them, and re-layouts, gather_four(): lax.dynamic_update_slice_in_dim(whole, jnp.expand_dims(part, dim), (me -...  13.2 us
    dot_general x5, matrix products, dot_over(): lax.dot_general(left, right, (((0,), (0,)), ((), ())), preferred_element_...  11.3 us
  transfers between devices with their start and end apart: 102, of which 50 were waited for; matrix products, arithmetic and copies ran while one was open for 16% of the time, Pallas kernels for 9%

profile of v1, /device:TPU:0, one launch (start us, length us, event | category | flops | bytes accessed | tf_op | source)
XLA Modules:
  0.0 515.7 jit_solution(10287099405793024238)
XLA Ops:
  6.3 2.1 collective-permute-start.29
  14.9 6.8 %collective-permute-done.10 = s32[2,1,128]{2,0,1:T(2,128)S(1)} collective-permute-done((s32[2,1,128]{2,0,1:T(2,128)}, s32[2,1,128]{2,0,1:T(2,128)S(1)}, u32[]{:S(2)}, u32[]{:S(2)}) %collective-permute-start.10) | collective-permute-done | bytes 1056 | tf_op jit(solution)/shard_map/ppermute | solution.py:27
  36.8 2.6 collective-permute-start.13
  42.3 5.0 collective-permute-done.14
  53.4 4.0 collective-permute-done.23
  65.5 4.0 collective-permute-done.5
  70.1 5.9 %collective-permute-done.18 = bf16[64,1024]{1,0:T(8,128)(2,1)S(1)} collective-permute-done((bf16[64,1024]{1,0:T(8,128)(2,1)S(1)}, bf16[64,1024]{1,0:T(8,128)(2,1)S(1)}, u32[]{:S(2)}, u32[]{:S(2)}) %collective-permute-start.18) | collective-permute-done | bytes 131104 | tf_op jit(solution)/shard_map/ppermute | solution.py:27
  76.1 4.9 collective-permute-done.19
  82.1 5.4 %collective-permute-done.20 = bf16[64,1024]{1,0:T(8,128)(2,1)S(1)} collective-permute-done((bf16[64,1024]{1,0:T(8,128)(2,1)S(1)}, bf16[64,1024]{1,0:T(8,128)(2,1)S(1)}, u32[]{:S(2)}, u32[]{:S(2)}) %collective-permute-start.20) | collective-permute-done | bytes 131104 | tf_op jit(solution)/shard_map/ppermute | solution.py:27
  89.5 7.2 %collective-permute-done.16 = bf16[4,64,512]{2,1,0:T(8,128)(2,1)S(1)} collective-permute-done((bf16[4,64,512]{2,1,0:T(8,128)(2,1)S(1)}, bf16[4,64,512]{2,1,0:T(8,128)(2,1)S(1)}, u32[]{:S(2)}, u32[]{:S(2)}) %collective-permute-start.16) | collective-permute-done | bytes 262176 | tf_op jit(solution)/shard_map/ppermute | solution.py:27
  99.5 2.6 maximum_select_fusion.2
  102.2 4.1 collective-permute-done.6
  106.6 7.5 %collective-permute-done.7 = bf16[4,64,384]{2,1,0:T(8,128)(2,1)S(1)} collective-permute-done((bf16[4,64,384]{2,1,0:T(8,128)(2,1)S(1)}, bf16[4,64,384]{2,1,0:T(8,128)(2,1)S(1)}, u32[]{:S(2)}, u32[]{:S(2)}) %collective-permute-start.7) | collective-permute-done | bytes 196640 | tf_op jit(solution)/shard_map/ppermute | solution.py:27
  115.1 6.2 %collective-permute-done.8 = bf16[4,64,384]{2,1,0:T(8,128)(2,1)S(1)} collective-permute-done((bf16[4,64,384]{2,1,0:T(8,128)(2,1)S(1)}, bf16[4,64,384]{2,1,0:T(8,128)(2,1)S(1)}, u32[]{:S(2)}, u32[]{:S(2)}) %collective-permute-start.8) | collective-permute-done | bytes 196640 | tf_op jit(solution)/shard_map/ppermute | solution.py:27
  121.3 3.6 collective-permute-start.25
  132.9 4.6 collective-permute-done.25
  141.6 10.8 %layer_forward.4 = bf16[2,256,1024]{2,1,0:T(8,128)(2,1)} custom-call(bf16[2,256,1024]{2,1,0:T(8,128)(2,1)} %get-tuple-element.134.hidden, s32[2,1,256]{2,1,0:T(1,128)} %get-tuple-element.199.seg_row, s32[2,256,1]{2,1,0:T(8,128)} %copy.123.seg_col, f32[2,256,128]{2,1,0:T(8,128)} %get-tuple-element.164.cosine, f32[2,256,128]{2,1,0:T(8,128)} %get-tuple-element.162.sine, ...), custom_call_target="tpu_custom_call" | custom-call | flops 3221225472 | bytes 8388608 | tf_op jit(solution)/shard_map/layer_forward/pallas_call | solution.py:270
  154.7 10.9 %layer_forward.6 = bf16[2,256,1024]{2,1,0:T(8,128)(2,1)} custom-call(bf16[2,256,1024]{2,1,0:T(8,128)(2,1)} %get-tuple-element.135.hidden, s32[2,1,256]{2,1,0:T(1,128)} %get-tuple-element.198.seg_row, s32[2,256,1]{2,1,0:T(8,128)} %broadcast_in_dim_squeeze.16.seg_col, f32[2,256,128]{2,1,0:T(8,128)} %get-tuple-element.165.cosine, ...), custom_call_target="tpu_custom_call" | custom-call | flops 3221225472 | bytes 8388608 | tf_op jit(solution)/shard_map/layer_forward/pallas_call | solution.py:270
  175.5 7.4 %collective-permute-done.47 = bf16[2,1,128,1024]{3,2,1,0:T(8,128)(2,1)} collective-permute-done((bf16[2,1,128,1024]{3,2,1,0:T(8,128)(2,1)S(1)}, bf16[2,1,128,1024]{3,2,1,0:T(8,128)(2,1)}, u32[]{:S(2)}, u32[]{:S(2)}) %collective-permute-start.47) | collective-permute-done | bytes 524320 | tf_op jit(solution)/shard_map/ppermute | solution.py:27
  184.7 3.8 collective-permute-done.34
  188.4 4.7 collective-permute-done.41
  195.1 5.8 %collective-permute-start.36 = (bf16[128,1024]{1,0:T(8,128)(2,1)S(1)}, bf16[128,1024]{1,0:T(8,128)(2,1)S(1)}, u32[]{:S(2)}, u32[]{:S(2)}) collective-permute-start(bf16[128,1024]{1,0:T(8,128)(2,1)S(1)} %get-tuple-element.136), channel_id=1, source_target_pairs={{0,96},{32,64},{1,97},{33,65},{2,98},{34,66},{3,99},{35,67},{4,100... | collective-permute-start | bytes 786440 | tf_op jit(solution)/shard_map/ppermute | solution.py:460
  205.0 13.8 %collective-permute-done.36 = bf16[128,1024]{1,0:T(8,128)(2,1)S(1)} collective-permute-done((bf16[128,1024]{1,0:T(8,128)(2,1)S(1)}, bf16[128,1024]{1,0:T(8,128)(2,1)S(1)}, u32[]{:S(2)}, u32[]{:S(2)}) %collective-permute-start.36) | collective-permute-done | bytes 262176 | tf_op jit(solution)/shard_map/ppermute | solution.py:460
  219.8 2.9 collective-permute-done.43
  224.7 2.0 maximum_select_fusion.1
  228.3 3.7 fusion.11
  232.0 11.3 %layer_forward.5 = (bf16[2,256,1024]{2,1,0:T(8,128)(2,1)}, bf16[2,256,1024]{2,1,0:T(8,128)(2,1)}, bf16[2,256,1024]{2,1,0:T(8,128)(2,1)}, bf16[2,256,256]{2,1,0:T...) custom-call(bf16[2,256,1024]{2,1,0:T(8,128)(2,1)} %get-tuple-element, ...), custom_call_target="tpu_custom_call" | custom-call | flops 3221225472 | bytes 8388608 | tf_op jit(solution)/shard_map/layer_forward/pallas_call | solution.py:270
  245.1 11.3 %layer_forward.7 = (bf16[2,256,1024]{2,1,0:T(8,128)(2,1)}, bf16[2,256,1024]{2,1,0:T(8,128)(2,1)}, bf16[2,256,1024]{2,1,0:T(8,128)(2,1)}, bf16[2,256,256]{2,1,0:T...) custom-call(bf16[2,256,1024]{2,1,0:T(8,128)(2,1)} %get-tuple-element, ...), custom_call_target="tpu_custom_call" | custom-call | flops 3221225472 | bytes 8388608 | tf_op jit(solution)/shard_map/layer_forward/pallas_call | solution.py:270
  256.4 13.3 %layer_backward.4 = bf16[2,256,1024]{2,1,0:T(8,128)(2,1)} custom-call(bf16[2,256,1024]{2,1,0:T(8,128)(2,1)} %get-tuple-element.130.grad, bf16[2,256,1024]{2,1,0:T(8,128)(2,1)} %get-tuple-element.132.hidden, s32[2,1,256]{2,1,0:T(1,128)} %get-tuple-element.199.seg_row, s32[2,256,1]{2,1,0:T(8,128)} %copy.123.seg_col, f32[2,256,128]{2,1,0:T(8,128)} %get-tuple-element.164.cosine, ...), custom_call_target="tpu_custom_call" | custom-call | flops 3221225472 | bytes 8388608 | tf_op jit(solution)/shard_map/layer_backward/pallas_call | solution.py:294
  270.9 13.3 %layer_backward.6 = bf16[2,256,1024]{2,1,0:T(8,128)(2,1)} custom-call(bf16[2,256,1024]{2,1,0:T(8,128)(2,1)} %get-tuple-element.131.grad, bf16[2,256,1024]{2,1,0:T(8,128)(2,1)} %get-tuple-element.133.hidden, s32[2,1,256]{2,1,0:T(1,128)} %get-tuple-element.198.seg_row, s32[2,256,1]{2,1,0:T(8,128)} %broadcast_in_dim_squeeze.16.seg_col, ...), custom_call_target="tpu_custom_call" | custom-call | flops 3221225472 | bytes 8388608 | tf_op jit(solution)/shard_map/layer_backward/pallas_call | solution.py:294
  290.2 6.0 %collective-permute-done.50 = bf16[128,1024]{1,0:T(8,128)(2,1)S(1)} collective-permute-done((bf16[128,1024]{1,0:T(8,128)(2,1)S(1)}, bf16[128,1024]{1,0:T(8,128)(2,1)S(1)}, u32[]{:S(2)}, u32[]{:S(2)}) %collective-permute-start.50) | collective-permute-done | bytes 262176 | tf_op jit(solution)/shard_map/ppermute | solution.py:27
  296.2 5.6 %collective-permute-done.57 = bf16[128,1024]{1,0:T(8,128)(2,1)S(1)} collective-permute-done((bf16[128,1024]{1,0:T(8,128)(2,1)S(1)}, bf16[128,1024]{1,0:T(8,128)(2,1)S(1)}, u32[]{:S(2)}, u32[]{:S(2)}) %collective-permute-start.57) | collective-permute-done | bytes 262176 | tf_op jit(solution)/shard_map/ppermute | solution.py:27
  307.7 18.0 %collective-permute-done.52 = bf16[128,1024]{1,0:T(8,128)(2,1)S(1)} collective-permute-done((bf16[128,1024]{1,0:T(8,128)(2,1)S(1)}, bf16[128,1024]{1,0:T(8,128)(2,1)S(1)}, u32[]{:S(2)}, u32[]{:S(2)}) %collective-permute-start.52) | collective-permute-done | bytes 262176 | tf_op jit(solution)/shard_map/ppermute | solution.py:460
  325.9 3.7 collective-permute-done.59
  334.8 13.7 %layer_backward.7 = (bf16[2,256,1024]{2,1,0:T(8,128)(2,1)}, bf16[2,256,1024]{2,1,0:T(8,128)(2,1)}, bf16[2,256,256]{2,1,0:T(8,128)(2,1)}, bf16[2,256,512]{2,1,0:T(8,128)(2,1)}, f32[2,8,1024]{2,1,0:T(8,128)}) custom-call(bf16[2,256,1024]{2,1,0:T(8,128)(2,1)} %get-tuple-element.129.grad, bf16[2,256,1024]{2,1,0:T(8,128)(2,1)} %get-tuple-element.133.hidden, ...), custom_call_target="tpu_custom_call" | custom-call | flops 3221225472 | bytes 8388608 | tf_op jit(solution)/shard_map/layer_backward/pallas_call | solution.py:294
  348.6 13.8 %layer_backward.5 = (bf16[2,256,1024]{2,1,0:T(8,128)(2,1)}, bf16[2,256,1024]{2,1,0:T(8,128)(2,1)}, bf16[2,256,256]{2,1,0:T(8,128)(2,1)}, bf16[2,256,512]{2,1,0:T(8,128)(2,1)}, f32[2,8,1024]{2,1,0:T(8,128)}) custom-call(bf16[2,256,1024]{2,1,0:T(8,128)(2,1)} %get-tuple-element.128.grad, bf16[2,256,1024]{2,1,0:T(8,128)(2,1)} %get-tuple-element.132.hidden, ...), custom_call_target="tpu_custom_call" | custom-call | flops 3221225472 | bytes 8388608 | tf_op jit(solution)/shard_map/layer_backward/pallas_call | solution.py:294
  368.9 2.3 fusion.9
  371.9 3.7 collective-permute-start.64
  376.5 4.6 bitcast_convert_fusion.1
  387.1 2.4 bitcast_convert_fusion
  391.2 2.1 collective-permute-start.81
  393.2 2.6 collective-permute-start.80
  396.0 2.5 collective-permute-done.81
  400.4 3.3 collective-permute-start.67
  404.1 3.1 collective-permute-start.73
  408.9 3.4 collective-permute-done.66
  413.7 3.6 collective-permute-done.70
  419.1 3.3 collective-permute-start.83
  422.4 6.5 %collective-permute-done.71 = bf16[4,64,512]{2,1,0:T(8,128)(2,1)S(1)} collective-permute-done((bf16[4,64,512]{2,1,0:T(8,128)(2,1)S(1)}, bf16[4,64,512]{2,1,0:T(8,128)(2,1)S(1)}, u32[]{:S(2)}, u32[]{:S(2)}) %collective-permute-start.71) | collective-permute-done | bytes 262176 | tf_op jit(solution)/shard_map/ppermute | solution.py:27
  429.2 2.9 collective-permute-start.76
  432.2 2.9 collective-permute-start.75
  435.2 3.1 collective-permute-start.74
  438.4 2.0 collective-permute-start.89
  441.2 2.1 collective-permute-done.74
  446.3 3.7 collective-permute-done.86
  450.9 3.7 collective-permute-done.78
  457.3 7.0 %collective-permute-start.97 = (bf16[4,64,1024]{2,1,0:T(8,128)(2,1)}, bf16[4,64,1024]{2,1,0:T(8,128)(2,1)S(1)}, u32[]{:S(2)}, u32[]{:S(2)}) collective-permute-start(bf16[4,64,1024]{2,1,0:T(8,128)(2,1)} %get-tuple-element.123), channel_id=1, source_target_pairs={{0,4},{2,6},{4,0},{6,2},{1,5},{3,7},{5,1},{7,3},{8,12},{10,14},{12... | collective-permute-start | bytes 1572872 | tf_op jit(solution)/shard_map/ppermute | solution.py:27
  465.5 2.3 collective-permute-start.96
  474.3 3.1 collective-permute-done.97
  477.4 3.5 collective-permute-start.92
  480.9 9.8 %collective-permute-done.96 = bf16[4,64,1024]{2,1,0:T(8,128)(2,1)S(1)} collective-permute-done((bf16[4,64,1024]{2,1,0:T(8,128)(2,1)}, bf16[4,64,1024]{2,1,0:T(8,128)(2,1)S(1)}, u32[]{:S(2)}, u32[]{:S(2)}) %collective-permute-start.96) | collective-permute-done | bytes 524320 | tf_op jit(solution)/shard_map/ppermute | solution.py:27
  490.7 2.6 collective-permute-start.91
  496.3 3.0 collective-permute-start.99
  501.5 3.1 collective-permute-done.99
  (498 shorter events, 162.1 us)
Async XLA Ops:
  3.1 26.2 %collective-permute-start.27 = (bf16[64,1024]{1,0:T(8,128)(2,1)S(1)}, bf16[64,1024]{1,0:T(8,128)(2,1)S(1)}, u32[]{:S(2)}, u32[]{:S(2)}) collective-permute-start(bf16[64,1024]{1,0:T(8,128)(2,1)S(1)} %get-tuple-element.179), channel_id=1, source_target_pairs={{0,8},{8,16},{16,24},{24,0},{1,9},{9,17},{17,25},{25,1},{2,10},{10... | collective-permute-start | bytes 393224 | tf_op jit(solution)/shard_map/ppermute | solution.py:27
  4.8 25.2 %collective-permute-start.28 = (bf16[64,1024]{1,0:T(8,128)(2,1)S(1)}, bf16[64,1024]{1,0:T(8,128)(2,1)S(1)}, u32[]{:S(2)}, u32[]{:S(2)}) collective-permute-start(bf16[64,1024]{1,0:T(8,128)(2,1)S(1)} %get-tuple-element.179), channel_id=1, source_target_pairs={{0,24},{8,0},{16,8},{24,16},{1,25},{9,1},{17,9},{25,17},{2,26},{10... | collective-permute-start | bytes 393224 | tf_op jit(solution)/shard_map/ppermute | solution.py:27
  6.3 24.3 %collective-permute-start.29 = (bf16[64,1024]{1,0:T(8,128)(2,1)S(1)}, bf16[64,1024]{1,0:T(8,128)(2,1)S(1)}, u32[]{:S(2)}, u32[]{:S(2)}) collective-permute-start(bf16[64,1024]{1,0:T(8,128)(2,1)S(1)} %get-tuple-element.179), channel_id=1, source_target_pairs={{0,16},{8,24},{16,0},{24,8},{1,17},{9,25},{17,1},{25,9},{2,18},{10... | collective-permute-start | bytes 393224 | tf_op jit(solution)/shard_map/ppermute | solution.py:27
  8.4 90.6 %collective-permute-start = (bf16[2,1,128,1024]{3,2,1,0:T(8,128)(2,1)}, bf16[2,1,128,1024]{3,2,1,0:T(8,128)(2,1)}, u32[]{:S(2)}, u32[]{:S(2)}) collective-permute-start(bf16[2,1,128,1024]{3,2,1,0:T(8,128)(2,1)} %param.16), channel_id=1, source_target_pairs={{0,32},{32,0},{1,33},{33,1},{2,34},{34,2},{3,35},{35,3},{4,36},{36... | collective-permute-start | bytes 1572872 | tf_op jit(solution)/shard_map/ppermute | solution.py:27
  10.3 11.4 %collective-permute-start.10 = (s32[2,1,128]{2,0,1:T(2,128)}, s32[2,1,128]{2,0,1:T(2,128)S(1)}, u32[]{:S(2)}, u32[]{:S(2)}) collective-permute-start(s32[2,1,128]{2,0,1:T(2,128)} %bitcast.586), channel_id=1, source_target_pairs={{0,32},{32,0},{1,33},{33,1},{2,34},{34,2},{3,35},{35,3},{4,36},{36... | collective-permute-start | bytes 3080 | tf_op jit(solution)/shard_map/ppermute | solution.py:27
  25.3 10.5 %collective-permute-start.2 = (bf16[32,2944]{1,0:T(8,128)(2,1)S(1)}, bf16[32,2944]{1,0:T(8,128)(2,1)S(1)}, u32[]{:S(2)}, u32[]{:S(2)}) collective-permute-start(bf16[32,2944]{1,0:T(8,128)(2,1)S(1)} %pad_maximum_fusion.6), channel_id=1, source_target_pairs={{0,1},{1,0},{2,3},{3,2},{4,5},{5,4},{6,7},{7,6},{8,9},{9,8},{10,11... | collective-permute-start | bytes 565256 | tf_op jit(solution)/shard_map/ppermute | solution.py:27
  31.3 96.4 %collective-permute-start.30 = (bf16[4,64,1024]{2,1,0:T(8,128)(2,1)}, bf16[4,64,1024]{2,1,0:T(8,128)(2,1)}, u32[]{:S(2)}, u32[]{:S(2)}) collective-permute-start(bf16[4,64,1024]{2,1,0:T(8,128)(2,1)} %bitcast_dynamic-update-slice_fusion.20), channel_id=1, source_target_pairs={{0,2},{2,4},{4,6},{6,0},{1,3},{3,5},{5,7},{7,1},{8,10},{10,12},{12... | collective-permute-start | bytes 1572872 | tf_op jit(solution)/shard_map/ppermute | solution.py:27
  32.8 96.3 %collective-permute-start.31 = (bf16[4,64,1024]{2,1,0:T(8,128)(2,1)}, bf16[4,64,1024]{2,1,0:T(8,128)(2,1)}, u32[]{:S(2)}, u32[]{:S(2)}) collective-permute-start(bf16[4,64,1024]{2,1,0:T(8,128)(2,1)} %bitcast_dynamic-update-slice_fusion.20), channel_id=1, source_target_pairs={{0,6},{2,0},{4,2},{6,4},{1,7},{3,1},{5,3},{7,5},{8,14},{10,8},{12,... | collective-permute-start | bytes 1572872 | tf_op jit(solution)/shard_map/ppermute | solution.py:27
  49.5 7.9 %collective-permute-start.23 = (bf16[64,1024]{1,0:T(8,128)(2,1)S(1)}, bf16[64,1024]{1,0:T(8,128)(2,1)S(1)}, u32[]{:S(2)}, u32[]{:S(2)}) collective-permute-start(bf16[64,1024]{1,0:T(8,128)(2,1)S(1)} %get-tuple-element.174), channel_id=1, source_target_pairs={{0,4},{2,6},{4,0},{6,2},{1,5},{3,7},{5,1},{7,3},{8,12},{10,14},{12... | collective-permute-start | bytes 393224 | tf_op jit(solution)/shard_map/ppermute | solution.py:27
  52.8 8.6 %collective-permute-start.3 = (bf16[64,1408]{1,0:T(8,128)(2,1)S(1)}, bf16[64,1408]{1,0:T(8,128)(2,1)S(1)}, u32[]{:S(2)}, u32[]{:S(2)}) collective-permute-start(bf16[64,1408]{1,0:T(8,128)(2,1)S(1)} %pad_maximum_fusion.7), channel_id=1, source_target_pairs={{0,2},{2,4},{4,6},{6,0},{1,3},{3,5},{5,7},{7,1},{8,10},{10,12},{12... | collective-permute-start | bytes 540680 | tf_op jit(solution)/shard_map/ppermute | solution.py:27
  61.3 8.2 %collective-permute-start.5 = (bf16[64,1408]{1,0:T(8,128)(2,1)S(1)}, bf16[64,1408]{1,0:T(8,128)(2,1)S(1)}, u32[]{:S(2)}, u32[]{:S(2)}) collective-permute-start(bf16[64,1408]{1,0:T(8,128)(2,1)S(1)} %pad_maximum_fusion.7), channel_id=1, source_target_pairs={{0,4},{2,6},{4,0},{6,2},{1,5},{3,7},{5,1},{7,3},{8,12},{10,14},{12... | collective-permute-start | bytes 540680 | tf_op jit(solution)/shard_map/ppermute | solution.py:27
  64.3 24.0 %collective-permute-start.15 = (bf16[4,64,512]{2,1,0:T(8,128)(2,1)S(1)}, bf16[4,64,512]{2,1,0:T(8,128)(2,1)S(1)}, u32[]{:S(2)}, u32[]{:S(2)}) collective-permute-start(bf16[4,64,512]{2,1,0:T(8,128)(2,1)S(1)} %bitcast_dynamic-update-slice_fusion.31), channel_id=1, source_target_pairs={{0,2},{2,4},{4,6},{6,0},{1,3},{3,5},{5,7},{7,1},{8,10},{10,12},{12... | collective-permute-start | bytes 786440 | tf_op jit(solution)/shard_map/ppermute | solution.py:27
  87.5 9.2 %collective-permute-start.16 = (bf16[4,64,512]{2,1,0:T(8,128)(2,1)S(1)}, bf16[4,64,512]{2,1,0:T(8,128)(2,1)S(1)}, u32[]{:S(2)}, u32[]{:S(2)}) collective-permute-start(bf16[4,64,512]{2,1,0:T(8,128)(2,1)S(1)} %bitcast_dynamic-update-slice_fusion.31), channel_id=1, source_target_pairs={{0,6},{2,0},{4,2},{6,4},{1,7},{3,1},{5,3},{7,5},{8,14},{10,8},{12,... | collective-permute-start | bytes 786440 | tf_op jit(solution)/shard_map/ppermute | solution.py:27
  88.3 10.3 %collective-permute-start.17 = (bf16[4,64,512]{2,1,0:T(8,128)(2,1)S(1)}, bf16[4,64,512]{2,1,0:T(8,128)(2,1)S(1)}, u32[]{:S(2)}, u32[]{:S(2)}) collective-permute-start(bf16[4,64,512]{2,1,0:T(8,128)(2,1)S(1)} %bitcast_dynamic-update-slice_fusion.31), channel_id=1, source_target_pairs={{0,4},{2,6},{4,0},{6,2},{1,5},{3,7},{5,1},{7,3},{8,12},{10,14},{12... | collective-permute-start | bytes 786440 | tf_op jit(solution)/shard_map/ppermute | solution.py:27
  96.7 33.5 %collective-permute-start.32 = (bf16[4,64,1024]{2,1,0:T(8,128)(2,1)}, bf16[4,64,1024]{2,1,0:T(8,128)(2,1)}, u32[]{:S(2)}, u32[]{:S(2)}) collective-permute-start(bf16[4,64,1024]{2,1,0:T(8,128)(2,1)} %bitcast_dynamic-update-slice_fusion.20), channel_id=1, source_target_pairs={{0,4},{2,6},{4,0},{6,2},{1,5},{3,7},{5,1},{7,3},{8,12},{10,14},{12... | collective-permute-start | bytes 1572872 | tf_op jit(solution)/shard_map/ppermute | solution.py:27
  99.1 32.4 %collective-permute-start.24 = (bf16[4,64,1024]{2,1,0:T(8,128)(2,1)}, bf16[4,64,1024]{2,1,0:T(8,128)(2,1)}, u32[]{:S(2)}, u32[]{:S(2)}) collective-permute-start(bf16[4,64,1024]{2,1,0:T(8,128)(2,1)} %bitcast_dynamic-update-slice_fusion.23), channel_id=1, source_target_pairs={{0,8},{8,16},{16,24},{24,0},{1,9},{9,17},{17,25},{25,1},{2,10},{10... | collective-permute-start | bytes 1572872 | tf_op jit(solution)/shard_map/ppermute | solution.py:27
  106.2 7.8 %collective-permute-start.7 = (bf16[4,64,384]{2,1,0:T(8,128)(2,1)S(1)}, bf16[4,64,384]{2,1,0:T(8,128)(2,1)S(1)}, u32[]{:S(2)}, u32[]{:S(2)}) collective-permute-start(bf16[4,64,384]{2,1,0:T(8,128)(2,1)S(1)} %slice.251), channel_id=1, source_target_pairs={{0,24},{8,0},{16,8},{24,16},{1,25},{9,1},{17,9},{25,17},{2,26},{10... | collective-permute-start | bytes 589832 | tf_op jit(solution)/shard_map/ppermute | solution.py:27
  121.3 16.3 %collective-permute-start.25 = (bf16[4,64,1024]{2,1,0:T(8,128)(2,1)}, bf16[4,64,1024]{2,1,0:T(8,128)(2,1)}, u32[]{:S(2)}, u32[]{:S(2)}) collective-permute-start(bf16[4,64,1024]{2,1,0:T(8,128)(2,1)} %bitcast_dynamic-update-slice_fusion.23), channel_id=1, source_target_pairs={{0,24},{8,0},{16,8},{24,16},{1,25},{9,1},{17,9},{25,17},{2,26},{10... | collective-permute-start | bytes 1572872 | tf_op jit(solution)/shard_map/ppermute | solution.py:27
  127.7 11.0 %collective-permute-start.26 = (bf16[4,64,1024]{2,1,0:T(8,128)(2,1)}, bf16[4,64,1024]{2,1,0:T(8,128)(2,1)S(1)}, u32[]{:S(2)}, u32[]{:S(2)}) collective-permute-start(bf16[4,64,1024]{2,1,0:T(8,128)(2,1)} %bitcast_dynamic-update-slice_fusion.23), channel_id=1, source_target_pairs={{0,16},{8,24},{16,0},{24,8},{1,17},{9,25},{17,1},{25,9},{2,18},{10... | collective-permute-start | bytes 1572872 | tf_op jit(solution)/shard_map/ppermute | solution.py:27
  129.1 9.6 %collective-permute-start.1 = (bf16[2,1,256,1024]{3,2,1,0:T(8,128)(2,1)}, bf16[2,1,256,1024]{3,2,1,0:T(8,128)(2,1)S(1)}, u32[]{:S(2)}, u32[]{:S(2)}) collective-permute-start(bf16[2,1,256,1024]{3,2,1,0:T(8,128)(2,1)} %maximum_select_fusion.2), channel_id=1, source_target_pairs={{0,1},{1,0},{2,3},{3,2},{4,5},{5,4},{6,7},{7,6},{8,9},{9,8},{10,11... | collective-permute-start | bytes 3145736 | tf_op jit(solution)/shard_map/ppermute | solution.py:27
  154.2 15.4 %collective-permute-start.33 = (bf16[256,1024]{1,0:T(8,128)(2,1)}, bf16[256,1024]{1,0:T(8,128)(2,1)}, u32[]{:S(2)}, u32[]{:S(2)}) collective-permute-start(bf16[256,1024]{1,0:T(8,128)(2,1)} %dynamic-slice_bitcast_fusion.13), channel_id=1, source_target_pairs={{0,1},{1,0},{2,3},{3,2},{4,5},{5,4},{6,7},{7,6},{8,9},{9,8},{10,11... | collective-permute-start | bytes 1572872 | tf_op jit(solution)/shard_map/ppermute | solution.py:27
  167.9 14.9 %collective-permute-start.47 = (bf16[2,1,128,1024]{3,2,1,0:T(8,128)(2,1)S(1)}, bf16[2,1,128,1024]{3,2,1,0:T(8,128)(2,1)}, u32[]{:S(2)}, u32[]{:S(2)}) collective-permute-start(bf16[2,1,128,1024]{3,2,1,0:T(8,128)(2,1)S(1)} %copy-done.20), channel_id=1, source_target_pairs={{0,32},{32,0},{1,33},{33,1},{2,34},{34,2},{3,35},{35,3},{4,36},{36... | collective-permute-start | bytes 1572872 | tf_op jit(solution)/shard_map/ppermute | solution.py:27
  171.2 17.2 %collective-permute-start.34 = (bf16[128,1024]{1,0:T(8,128)(2,1)S(1)}, bf16[128,1024]{1,0:T(8,128)(2,1)}, u32[]{:S(2)}, u32[]{:S(2)}) collective-permute-start(bf16[128,1024]{1,0:T(8,128)(2,1)S(1)} %fusion.53), channel_id=1, source_target_pairs={{0,32},{32,0},{1,33},{33,1},{2,34},{34,2},{3,35},{35,3},{4,36},{36... | collective-permute-start | bytes 786440 | tf_op jit(solution)/shard_map/ppermute | solution.py:27
  172.5 20.6 %collective-permute-start.41 = (bf16[128,1024]{1,0:T(8,128)(2,1)}, bf16[128,1024]{1,0:T(8,128)(2,1)}, u32[]{:S(2)}, u32[]{:S(2)}) collective-permute-start(bf16[128,1024]{1,0:T(8,128)(2,1)} %fusion.55), channel_id=1, source_target_pairs={{0,32},{32,0},{1,33},{33,1},{2,34},{34,2},{3,35},{35,3},{4,36},{36... | collective-permute-start | bytes 786440 | tf_op jit(solution)/shard_map/ppermute | solution.py:27
  184.5 40.2 %collective-permute-start.48 = (bf16[2,1,256,1024]{3,2,1,0:T(8,128)(2,1)S(1)}, bf16[2,1,256,1024]{3,2,1,0:T(8,128)(2,1)}, u32[]{:S(2)}, u32[]{:S(2)}) collective-permute-start(bf16[2,1,256,1024]{3,2,1,0:T(8,128)(2,1)S(1)} %maximum_select_fusion.5), channel_id=1, source_target_pairs={{0,1},{1,0},{2,3},{3,2},{4,5},{5,4},{6,7},{7,6},{8,9},{9,8},{10,11... | collective-permute-start | bytes 3145736 | tf_op jit(solution)/shard_map/ppermute | solution.py:27
  195.1 23.7 %collective-permute-start.36 = (bf16[128,1024]{1,0:T(8,128)(2,1)S(1)}, bf16[128,1024]{1,0:T(8,128)(2,1)S(1)}, u32[]{:S(2)}, u32[]{:S(2)}) collective-permute-start(bf16[128,1024]{1,0:T(8,128)(2,1)S(1)} %get-tuple-element.136), channel_id=1, source_target_pairs={{0,96},{32,64},{1,97},{33,65},{2,98},{34,66},{3,99},{35,67},{4,100... | collective-permute-start | bytes 786440 | tf_op jit(solution)/shard_map/ppermute | solution.py:460
  200.9 17.9 %collective-permute-start.35 = (bf16[128,1024]{1,0:T(8,128)(2,1)S(1)}, bf16[128,1024]{1,0:T(8,128)(2,1)S(1)}, u32[]{:S(2)}, u32[]{:S(2)}) collective-permute-start(bf16[128,1024]{1,0:T(8,128)(2,1)S(1)} %get-tuple-element.136), channel_id=1, source_target_pairs={{0,64},{32,96},{1,65},{33,97},{2,66},{34,98},{3,67},{35,99},{4,68}... | collective-permute-start | bytes 786440 | tf_op jit(solution)/shard_map/ppermute | solution.py:457
  202.3 20.4 %collective-permute-start.43 = (bf16[128,1024]{1,0:T(8,128)(2,1)S(1)}, bf16[128,1024]{1,0:T(8,128)(2,1)S(1)}, u32[]{:S(2)}, u32[]{:S(2)}) collective-permute-start(bf16[128,1024]{1,0:T(8,128)(2,1)S(1)} %get-tuple-element.137), channel_id=1, source_target_pairs={{0,96},{32,64},{1,97},{33,65},{2,98},{34,66},{3,99},{35,67},{4,100... | collective-permute-start | bytes 786440 | tf_op jit(solution)/shard_map/ppermute | solution.py:460
  203.6 19.1 %collective-permute-start.42 = (bf16[128,1024]{1,0:T(8,128)(2,1)S(1)}, bf16[128,1024]{1,0:T(8,128)(2,1)S(1)}, u32[]{:S(2)}, u32[]{:S(2)}) collective-permute-start(bf16[128,1024]{1,0:T(8,128)(2,1)S(1)} %get-tuple-element.137), channel_id=1, source_target_pairs={{0,64},{32,96},{1,65},{33,97},{2,66},{34,98},{3,67},{35,99},{4,68}... | collective-permute-start | bytes 786440 | tf_op jit(solution)/shard_map/ppermute | solution.py:457
  219.8 8.6 %collective-permute-start.37 = (bf16[1,256,1024]{2,1,0:T(8,128)(2,1)}, bf16[1,256,1024]{2,1,0:T(8,128)(2,1)}, u32[]{:S(2)}, u32[]{:S(2)}) collective-permute-start(bf16[1,256,1024]{2,1,0:T(8,128)(2,1)} %maximum_select_fusion.8), channel_id=1, source_target_pairs={{0,1},{1,0},{2,3},{3,2},{4,5},{5,4},{6,7},{7,6},{8,9},{9,8},{10,11... | collective-permute-start | bytes 1572872 | tf_op jit(solution)/shard_map/ppermute | solution.py:27
  244.4 45.1 %collective-permute-start.38 = (bf16[256,1024]{1,0:T(8,128)(2,1)S(1)}, bf16[256,1024]{1,0:T(8,128)(2,1)S(1)}, u32[]{:S(2)}, u32[]{:S(2)}) collective-permute-start(bf16[256,1024]{1,0:T(8,128)(2,1)S(1)} %dynamic-slice_bitcast_fusion.12), channel_id=1, source_target_pairs={{0,1},{1,0},{2,3},{3,2},{4,5},{5,4},{6,7},{7,6},{8,9},{9,8},{10,11... | collective-permute-start | bytes 1572872 | tf_op jit(solution)/shard_map/ppermute | solution.py:27
  270.8 15.6 %collective-permute-start.49 = (bf16[256,1024]{1,0:T(8,128)(2,1)S(1)}, bf16[256,1024]{1,0:T(8,128)(2,1)S(1)}, u32[]{:S(2)}, u32[]{:S(2)}) collective-permute-start(bf16[256,1024]{1,0:T(8,128)(2,1)S(1)} %dynamic-slice_bitcast_fusion.9), channel_id=1, source_target_pairs={{0,1},{1,0},{2,3},{3,2},{4,5},{5,4},{6,7},{7,6},{8,9},{9,8},{10,11... | collective-permute-start | bytes 1572872 | tf_op jit(solution)/shard_map/ppermute | solution.py:27
  286.1 20.0 %collective-permute-start.45 = (bf16[256,1024]{1,0:T(8,128)(2,1)S(1)}, bf16[256,1024]{1,0:T(8,128)(2,1)S(1)}, u32[]{:S(2)}, u32[]{:S(2)}) collective-permute-start(bf16[256,1024]{1,0:T(8,128)(2,1)S(1)} %dynamic-slice_bitcast_fusion.10), channel_id=1, source_target_pairs={{0,1},{1,0},{2,3},{3,2},{4,5},{5,4},{6,7},{7,6},{8,9},{9,8},{10,11... | collective-permute-start | bytes 1572872 | tf_op jit(solution)/shard_map/ppermute | solution.py:27
  287.0 9.2 %collective-permute-start.50 = (bf16[128,1024]{1,0:T(8,128)(2,1)S(1)}, bf16[128,1024]{1,0:T(8,128)(2,1)S(1)}, u32[]{:S(2)}, u32[]{:S(2)}) collective-permute-start(bf16[128,1024]{1,0:T(8,128)(2,1)S(1)} %fusion.57), channel_id=1, source_target_pairs={{0,32},{32,0},{1,33},{33,1},{2,34},{34,2},{3,35},{35,3},{4,36},{36... | collective-permute-start | bytes 786440 | tf_op jit(solution)/shard_map/ppermute | solution.py:27
  287.8 14.0 %collective-permute-start.57 = (bf16[128,1024]{1,0:T(8,128)(2,1)S(1)}, bf16[128,1024]{1,0:T(8,128)(2,1)S(1)}, u32[]{:S(2)}, u32[]{:S(2)}) collective-permute-start(bf16[128,1024]{1,0:T(8,128)(2,1)S(1)} %fusion.59), channel_id=1, source_target_pairs={{0,32},{32,0},{1,33},{33,1},{2,34},{34,2},{3,35},{35,3},{4,36},{36... | collective-permute-start | bytes 786440 | tf_op jit(solution)/shard_map/ppermute | solution.py:27
  289.7 40.8 %collective-permute-start.39 = (bf16[128,1024]{1,0:T(8,128)(2,1)S(1)}, bf16[128,1024]{1,0:T(8,128)(2,1)S(1)}, u32[]{:S(2)}, u32[]{:S(2)}) collective-permute-start(bf16[128,1024]{1,0:T(8,128)(2,1)S(1)} %fusion.54), channel_id=1, source_target_pairs={{0,32},{32,0},{1,33},{33,1},{2,34},{34,2},{3,35},{35,3},{4,36},{36... | collective-permute-start | bytes 786440 | tf_op jit(solution)/shard_map/ppermute | solution.py:27
  302.1 23.6 %collective-permute-start.52 = (bf16[128,1024]{1,0:T(8,128)(2,1)S(1)}, bf16[128,1024]{1,0:T(8,128)(2,1)S(1)}, u32[]{:S(2)}, u32[]{:S(2)}) collective-permute-start(bf16[128,1024]{1,0:T(8,128)(2,1)S(1)} %get-tuple-element.141), channel_id=1, source_target_pairs={{64,32},{96,0},{65,33},{97,1},{66,34},{98,2},{67,35},{99,3},{68,36... | collective-permute-start | bytes 786440 | tf_op jit(solution)/shard_map/ppermute | solution.py:460
  303.4 22.3 %collective-permute-start.51 = (bf16[128,1024]{1,0:T(8,128)(2,1)S(1)}, bf16[128,1024]{1,0:T(8,128)(2,1)S(1)}, u32[]{:S(2)}, u32[]{:S(2)}) collective-permute-start(bf16[128,1024]{1,0:T(8,128)(2,1)S(1)} %get-tuple-element.141), channel_id=1, source_target_pairs={{64,0},{96,32},{65,1},{97,33},{66,2},{98,34},{67,3},{99,35},{68,4}... | collective-permute-start | bytes 786440 | tf_op jit(solution)/shard_map/ppermute | solution.py:457
  304.7 24.9 %collective-permute-start.59 = (bf16[128,1024]{1,0:T(8,128)(2,1)S(1)}, bf16[128,1024]{1,0:T(8,128)(2,1)S(1)}, u32[]{:S(2)}, u32[]{:S(2)}) collective-permute-start(bf16[128,1024]{1,0:T(8,128)(2,1)S(1)} %get-tuple-element.142), channel_id=1, source_target_pairs={{64,32},{96,0},{65,33},{97,1},{66,34},{98,2},{67,35},{99,3},{68,36... | collective-permute-start | bytes 786440 | tf_op jit(solution)/shard_map/ppermute | solution.py:460
  306.2 23.5 %collective-permute-start.58 = (bf16[128,1024]{1,0:T(8,128)(2,1)S(1)}, bf16[128,1024]{1,0:T(8,128)(2,1)S(1)}, u32[]{:S(2)}, u32[]{:S(2)}) collective-permute-start(bf16[128,1024]{1,0:T(8,128)(2,1)S(1)} %get-tuple-element.142), channel_id=1, source_target_pairs={{64,0},{96,32},{65,1},{97,33},{66,2},{98,34},{67,3},{99,35},{68,4}... | collective-permute-start | bytes 786440 | tf_op jit(solution)/shard_map/ppermute | solution.py:457
  365.2 92.1 %collective-permute-start.61 = (bf16[256,1024]{1,0:T(8,128)(2,1)}, bf16[256,1024]{1,0:T(8,128)(2,1)}, u32[]{:S(2)}, u32[]{:S(2)}) collective-permute-start(bf16[256,1024]{1,0:T(8,128)(2,1)} %dynamic-slice_bitcast_fusion.6), channel_id=1, source_target_pairs={{0,1},{1,0},{2,3},{3,2},{4,5},{5,4},{6,7},{7,6},{8,9},{9,8},{10,11... | collective-permute-start | bytes 1572872 | tf_op jit(solution)/shard_map/ppermute | solution.py:27
  367.0 98.5 %collective-permute-start.54 = (bf16[256,1024]{1,0:T(8,128)(2,1)}, bf16[256,1024]{1,0:T(8,128)(2,1)}, u32[]{:S(2)}, u32[]{:S(2)}) collective-permute-start(bf16[256,1024]{1,0:T(8,128)(2,1)} %dynamic-slice_bitcast_fusion.8), channel_id=1, source_target_pairs={{0,1},{1,0},{2,3},{3,2},{4,5},{5,4},{6,7},{7,6},{8,9},{9,8},{10,11... | collective-permute-start | bytes 1572872 | tf_op jit(solution)/shard_map/ppermute | solution.py:27
  371.7 19.5 %collective-permute-start.65 = (bf16[4,64,384]{2,1,0:T(8,128)(2,1)S(1)}, bf16[4,64,384]{2,1,0:T(8,128)(2,1)S(1)}, u32[]{:S(2)}, u32[]{:S(2)}) collective-permute-start(bf16[4,64,384]{2,1,0:T(8,128)(2,1)S(1)} %get-tuple-element.146), channel_id=1, source_target_pairs={{0,16},{8,24},{16,0},{24,8},{1,17},{9,25},{17,1},{25,9},{2,18},{10... | collective-permute-start | bytes 589832 | tf_op jit(solution)/shard_map/ppermute | solution.py:27
  371.9 21.4 %collective-permute-start.64 = (bf16[4,64,384]{2,1,0:T(8,128)(2,1)S(1)}, bf16[4,64,384]{2,1,0:T(8,128)(2,1)S(1)}, u32[]{:S(2)}, u32[]{:S(2)}) collective-permute-start(bf16[4,64,384]{2,1,0:T(8,128)(2,1)S(1)} %get-tuple-element.147), channel_id=1, source_target_pairs={{0,24},{8,0},{16,8},{24,16},{1,25},{9,1},{17,9},{25,17},{2,26},{10... | collective-permute-start | bytes 589832 | tf_op jit(solution)/shard_map/ppermute | solution.py:27
  375.6 20.3 %collective-permute-start.63 = (bf16[4,64,384]{2,1,0:T(8,128)(2,1)S(1)}, bf16[4,64,384]{2,1,0:T(8,128)(2,1)S(1)}, u32[]{:S(2)}, u32[]{:S(2)}) collective-permute-start(bf16[4,64,384]{2,1,0:T(8,128)(2,1)S(1)} %get-tuple-element.145), channel_id=1, source_target_pairs={{0,8},{8,16},{16,24},{24,0},{1,9},{9,17},{17,25},{25,1},{2,10},{10... | collective-permute-start | bytes 589832 | tf_op jit(solution)/shard_map/ppermute | solution.py:27
  403.6 8.7 %collective-permute-start.66 = (bf16[64,384]{1,0:T(8,128)(2,1)S(1)}, bf16[64,384]{1,0:T(8,128)(2,1)S(1)}, u32[]{:S(2)}, u32[]{:S(2)}) collective-permute-start(bf16[64,384]{1,0:T(8,128)(2,1)S(1)} %get-tuple-element.181), channel_id=1, source_target_pairs={{0,2},{2,4},{4,6},{6,0},{1,3},{3,5},{5,7},{7,1},{8,10},{10,12},{12... | collective-permute-start | bytes 147464 | tf_op jit(solution)/shard_map/ppermute | solution.py:27
  404.1 14.9 %collective-permute-start.73 = (bf16[4,64,512]{2,1,0:T(8,128)(2,1)S(1)}, bf16[4,64,512]{2,1,0:T(8,128)(2,1)S(1)}, u32[]{:S(2)}, u32[]{:S(2)}) collective-permute-start(bf16[4,64,512]{2,1,0:T(8,128)(2,1)S(1)} %get-tuple-element.139), channel_id=1, source_target_pairs={{0,4},{2,6},{4,0},{6,2},{1,5},{3,7},{5,1},{7,3},{8,12},{10,14},{12... | collective-permute-start | bytes 786440 | tf_op jit(solution)/shard_map/ppermute | solution.py:27
  407.2 11.8 %collective-permute-start.72 = (bf16[4,64,512]{2,1,0:T(8,128)(2,1)S(1)}, bf16[4,64,512]{2,1,0:T(8,128)(2,1)S(1)}, u32[]{:S(2)}, u32[]{:S(2)}) collective-permute-start(bf16[4,64,512]{2,1,0:T(8,128)(2,1)S(1)} %get-tuple-element.140), channel_id=1, source_target_pairs={{0,6},{2,0},{4,2},{6,4},{1,7},{3,1},{5,3},{7,5},{8,14},{10,8},{12,... | collective-permute-start | bytes 786440 | tf_op jit(solution)/shard_map/ppermute | solution.py:27
  417.3 11.5 %collective-permute-start.71 = (bf16[4,64,512]{2,1,0:T(8,128)(2,1)S(1)}, bf16[4,64,512]{2,1,0:T(8,128)(2,1)S(1)}, u32[]{:S(2)}, u32[]{:S(2)}) collective-permute-start(bf16[4,64,512]{2,1,0:T(8,128)(2,1)S(1)} %get-tuple-element.138), channel_id=1, source_target_pairs={{0,2},{2,4},{4,6},{6,0},{1,3},{3,5},{5,7},{7,1},{8,10},{10,12},{12... | collective-permute-start | bytes 786440 | tf_op jit(solution)/shard_map/ppermute | solution.py:27
  419.0 10.2 %collective-permute-start.84 = (bf16[64,1024]{1,0:T(8,128)(2,1)S(1)}, bf16[64,1024]{1,0:T(8,128)(2,1)S(1)}, u32[]{:S(2)}, u32[]{:S(2)}) collective-permute-start(bf16[64,1024]{1,0:T(8,128)(2,1)S(1)} %get-tuple-element.157), channel_id=1, source_target_pairs={{0,4},{2,6},{4,0},{6,2},{1,5},{3,7},{5,1},{7,3},{8,12},{10,14},{12... | collective-permute-start | bytes 393224 | tf_op jit(solution)/shard_map/ppermute | solution.py:27
  419.1 13.1 %collective-permute-start.83 = (bf16[64,1024]{1,0:T(8,128)(2,1)S(1)}, bf16[64,1024]{1,0:T(8,128)(2,1)S(1)}, u32[]{:S(2)}, u32[]{:S(2)}) collective-permute-start(bf16[64,1024]{1,0:T(8,128)(2,1)S(1)} %get-tuple-element.158), channel_id=1, source_target_pairs={{0,6},{2,0},{4,2},{6,4},{1,7},{3,1},{5,3},{7,5},{8,14},{10,8},{12,... | collective-permute-start | bytes 393224 | tf_op jit(solution)/shard_map/ppermute | solution.py:27
  429.2 9.2 %collective-permute-start.76 = (bf16[64,512]{1,0:T(8,128)(2,1)S(1)}, bf16[64,512]{1,0:T(8,128)(2,1)S(1)}, u32[]{:S(2)}, u32[]{:S(2)}) collective-permute-start(bf16[64,512]{1,0:T(8,128)(2,1)S(1)} %get-tuple-element.177), channel_id=1, source_target_pairs={{0,16},{8,24},{16,0},{24,8},{1,17},{9,25},{17,1},{25,9},{2,18},{10... | collective-permute-start | bytes 196616 | tf_op jit(solution)/shard_map/ppermute | solution.py:27
  432.2 8.3 %collective-permute-start.75 = (bf16[64,512]{1,0:T(8,128)(2,1)S(1)}, bf16[64,512]{1,0:T(8,128)(2,1)S(1)}, u32[]{:S(2)}, u32[]{:S(2)}) collective-permute-start(bf16[64,512]{1,0:T(8,128)(2,1)S(1)} %get-tuple-element.178), channel_id=1, source_target_pairs={{0,24},{8,0},{16,8},{24,16},{1,25},{9,1},{17,9},{25,17},{2,26},{10... | collective-permute-start | bytes 196616 | tf_op jit(solution)/shard_map/ppermute | solution.py:27
  435.2 8.0 %collective-permute-start.74 = (bf16[64,512]{1,0:T(8,128)(2,1)S(1)}, bf16[64,512]{1,0:T(8,128)(2,1)S(1)}, u32[]{:S(2)}, u32[]{:S(2)}) collective-permute-start(bf16[64,512]{1,0:T(8,128)(2,1)S(1)} %get-tuple-element.176), channel_id=1, source_target_pairs={{0,8},{8,16},{16,24},{24,0},{1,9},{9,17},{17,25},{25,1},{2,10},{10... | collective-permute-start | bytes 196616 | tf_op jit(solution)/shard_map/ppermute | solution.py:27
  438.4 30.8 %collective-permute-start.89 = (bf16[4,64,1024]{2,1,0:T(8,128)(2,1)}, bf16[4,64,1024]{2,1,0:T(8,128)(2,1)}, u32[]{:S(2)}, u32[]{:S(2)}) collective-permute-start(bf16[4,64,1024]{2,1,0:T(8,128)(2,1)} %get-tuple-element.126), channel_id=1, source_target_pairs={{0,16},{8,24},{16,0},{24,8},{1,17},{9,25},{17,1},{25,9},{2,18},{10... | collective-permute-start | bytes 1572872 | tf_op jit(solution)/shard_map/ppermute | solution.py:27
  440.4 29.8 %collective-permute-start.88 = (bf16[4,64,1024]{2,1,0:T(8,128)(2,1)}, bf16[4,64,1024]{2,1,0:T(8,128)(2,1)}, u32[]{:S(2)}, u32[]{:S(2)}) collective-permute-start(bf16[4,64,1024]{2,1,0:T(8,128)(2,1)} %get-tuple-element.127), channel_id=1, source_target_pairs={{0,24},{8,0},{16,8},{24,16},{1,25},{9,1},{17,9},{25,17},{2,26},{10... | collective-permute-start | bytes 1572872 | tf_op jit(solution)/shard_map/ppermute | solution.py:27
  454.6 16.7 %collective-permute-start.87 = (bf16[4,64,1024]{2,1,0:T(8,128)(2,1)}, bf16[4,64,1024]{2,1,0:T(8,128)(2,1)}, u32[]{:S(2)}, u32[]{:S(2)}) collective-permute-start(bf16[4,64,1024]{2,1,0:T(8,128)(2,1)} %get-tuple-element.125), channel_id=1, source_target_pairs={{0,8},{8,16},{16,24},{24,0},{1,9},{9,17},{17,25},{25,1},{2,10},{10... | collective-permute-start | bytes 1572872 | tf_op jit(solution)/shard_map/ppermute | solution.py:27
  457.3 20.1 %collective-permute-start.97 = (bf16[4,64,1024]{2,1,0:T(8,128)(2,1)}, bf16[4,64,1024]{2,1,0:T(8,128)(2,1)S(1)}, u32[]{:S(2)}, u32[]{:S(2)}) collective-permute-start(bf16[4,64,1024]{2,1,0:T(8,128)(2,1)} %get-tuple-element.123), channel_id=1, source_target_pairs={{0,4},{2,6},{4,0},{6,2},{1,5},{3,7},{5,1},{7,3},{8,12},{10,14},{12... | collective-permute-start | bytes 1572872 | tf_op jit(solution)/shard_map/ppermute | solution.py:27
  465.5 25.2 %collective-permute-start.96 = (bf16[4,64,1024]{2,1,0:T(8,128)(2,1)}, bf16[4,64,1024]{2,1,0:T(8,128)(2,1)S(1)}, u32[]{:S(2)}, u32[]{:S(2)}) collective-permute-start(bf16[4,64,1024]{2,1,0:T(8,128)(2,1)} %get-tuple-element.124), channel_id=1, source_target_pairs={{0,6},{2,0},{4,2},{6,4},{1,7},{3,1},{5,3},{7,5},{8,14},{10,8},{12,... | collective-permute-start | bytes 1572872 | tf_op jit(solution)/shard_map/ppermute | solution.py:27
  469.2 24.1 %collective-permute-start.95 = (bf16[4,64,1024]{2,1,0:T(8,128)(2,1)S(1)}, bf16[4,64,1024]{2,1,0:T(8,128)(2,1)S(1)}, u32[]{:S(2)}, u32[]{:S(2)}) collective-permute-start(bf16[4,64,1024]{2,1,0:T(8,128)(2,1)S(1)} %get-tuple-element.122), channel_id=1, source_target_pairs={{0,2},{2,4},{4,6},{6,0},{1,3},{3,5},{5,7},{7,1},{8,10},{10,12},{12... | collective-permute-start | bytes 1572872 | tf_op jit(solution)/shard_map/ppermute | solution.py:27
  470.2 38.2 %collective-permute-start.62 = (bf16[128,1024]{1,0:T(8,128)(2,1)S(1)}, bf16[128,1024]{1,0:T(8,128)(2,1)S(1)}, u32[]{:S(2)}, u32[]{:S(2)}) collective-permute-start(bf16[128,1024]{1,0:T(8,128)(2,1)S(1)} %fusion.60), channel_id=1, source_target_pairs={{0,32},{32,0},{1,33},{33,1},{2,34},{34,2},{3,35},{35,3},{4,36},{36... | collective-permute-start | bytes 786440 | tf_op jit(solution)/shard_map/ppermute | solution.py:27
  471.3 37.2 %collective-permute-start.55 = (bf16[128,1024]{1,0:T(8,128)(2,1)S(1)}, bf16[128,1024]{1,0:T(8,128)(2,1)S(1)}, u32[]{:S(2)}, u32[]{:S(2)}) collective-permute-start(bf16[128,1024]{1,0:T(8,128)(2,1)S(1)} %fusion.58), channel_id=1, source_target_pairs={{0,32},{32,0},{1,33},{33,1},{2,34},{34,2},{3,35},{35,3},{4,36},{36... | collective-permute-start | bytes 786440 | tf_op jit(solution)/shard_map/ppermute | solution.py:27
  477.4 17.4 %collective-permute-start.92 = (bf16[64,1024]{1,0:T(8,128)(2,1)S(1)}, bf16[64,1024]{1,0:T(8,128)(2,1)S(1)}, u32[]{:S(2)}, u32[]{:S(2)}) collective-permute-start(bf16[64,1024]{1,0:T(8,128)(2,1)S(1)} %get-tuple-element.154), channel_id=1, source_target_pairs={{0,4},{2,6},{4,0},{6,2},{1,5},{3,7},{5,1},{7,3},{8,12},{10,14},{12... | collective-permute-start | bytes 393224 | tf_op jit(solution)/shard_map/ppermute | solution.py:27
  496.3 8.4 %collective-permute-start.99 = (bf16[64,1024]{1,0:T(8,128)(2,1)S(1)}, bf16[64,1024]{1,0:T(8,128)(2,1)S(1)}, u32[]{:S(2)}, u32[]{:S(2)}) collective-permute-start(bf16[64,1024]{1,0:T(8,128)(2,1)S(1)} %get-tuple-element.152), channel_id=1, source_target_pairs={{0,24},{8,0},{16,8},{24,16},{1,25},{9,1},{17,9},{25,17},{2,26},{10... | collective-permute-start | bytes 393224 | tf_op jit(solution)/shard_map/ppermute | solution.py:27
  (94 other events, 612.5 us)
